TPU v7x, 128 devices: a whole 4x4x4 slice. The times are simulated.
128 devices in a mesh: band: 32 (over x, y, core), patch: 4 (over z).
Axes of the slice: x: 4, y: 4, z: 4, core: 2. Of those that a mesh axis runs over, the one named last changes fastest.
Arguments:
- grid_feat: bfloat16 [262144, 227], P(('band', 'patch')), may hold values from -6 to 6
- w_embed: bfloat16 [227, 512], replicated, may hold values from -0.375 to 0.375
- w_send: bfloat16 [512, 512], replicated, may hold values from -0.25 to 0.25
- edge_vec: bfloat16 [512], replicated, may hold values from -5 to 5
- g2m_sender: int32 [128, 4096], P(('band', 'patch')), may hold values from 0 to 2047
- g2m_weight: float32 [128, 4096], P(('band', 'patch')), may hold values from 0.25 to 4
- g2m_target: int32 [128, 4096], P(('band', 'patch')), may hold values from -1 to 1023, as said below
- w_agg: bfloat16 [512, 512], replicated, may hold values from -0.25 to 0.25
- halo_rows: int32 [128, 4, 128], P(('band', 'patch')), may hold values from 0 to 1023
- mesh_src: int32 [131072, 6], P(('band', 'patch')), may hold values from 0 to 1535
- w_src: bfloat16 [2, 512, 512], replicated, may hold values from -0.25 to 0.25
- w_dst: bfloat16 [2, 512, 512], replicated, may hold values from -0.25 to 0.25
- w_up: bfloat16 [2, 1024, 512], replicated, may hold values from -0.1875 to 0.1875
- w_down: bfloat16 [2, 512, 512], replicated, may hold values from -0.25 to 0.25
- ln_gain: float32 [2, 512], replicated, may hold values from 0.1 to 1.9
Outputs:
- mesh_out: bfloat16 [131072, 512], P(('band', 'patch'))
Inputs may be any that keep to these rules, and one draw needn't show every extreme that they name: `g2m_target`: -1 marks an empty slot; other values are mesh rows of the receiving block. `halo_rows`: rows of the sending block. `mesh_src`: rows of the receiving block's extended table.
All inputs are finite; a program needn't handle non-finite values.
Results may differ from a plain program's by a relative error of at most 0.009.
Values may be sent and summed in bfloat16 or wider, within the bound.
A program may use at most 64 MiB of HBM per device.

v0:
```python
import jax
import jax.numpy as jnp
from jax import lax
from jax.sharding import PartitionSpec as P


def passed_along(x, axis, by):
    count = lax.axis_size(axis)
    return lax.ppermute(x, axis, [(i, (i + by) % count) for i in range(count)])


def passed_along_2(x, axis, by):
    count = lax.axis_size(axis)
    pairs = [(i, i + by) for i in range(count) if 0 <= i + by < count]
    return lax.ppermute(x, axis, pairs)


def patch_rim(rim_rows, offset):
    return passed_along(rim_rows, "patch", offset)


def band_rim(rim_rows, offset):
    return passed_along_2(rim_rows, "band", offset)


def node_update(extended, own_rows, sources_first, w_src_l, w_dst_l, w_up_l, w_down_l, gain_l):
    latent_width = own_rows.shape[1]
    degree, mesh_rows = sources_first.shape
    chosen_rows = jnp.take(extended, sources_first.reshape(-1), axis=0)
    from_send = jnp.dot(chosen_rows, w_src_l, preferred_element_type=jnp.float32).reshape(
        degree, mesh_rows, latent_width
    )
    at_recv = jnp.dot(own_rows, w_dst_l, preferred_element_type=jnp.float32)
    edge_sum = jnp.sum(jax.nn.silu(from_send + at_recv[None, :, :]), axis=0).astype(jnp.bfloat16)
    hidden = jax.nn.silu(
        jnp.dot(own_rows, w_up_l[:latent_width], preferred_element_type=jnp.float32)
        + jnp.dot(edge_sum, w_up_l[latent_width:], preferred_element_type=jnp.float32)
    ).astype(jnp.bfloat16)
    mixed = jnp.dot(hidden, w_down_l, preferred_element_type=jnp.float32)
    centre = mixed - jnp.mean(mixed, axis=1, keepdims=True)
    spread = jnp.mean(centre * centre, axis=1, keepdims=True)
    normed = centre * lax.rsqrt(spread + 1e-05) * gain_l[None, :]
    return (own_rows.astype(jnp.float32) + normed).astype(jnp.bfloat16)


def on_device(
    grid_feat,
    w_embed,
    w_send,
    edge_vec,
    g2m_sender,
    g2m_weight,
    g2m_target,
    w_agg,
    halo_rows,
    mesh_src,
    w_src,
    w_dst,
    w_up,
    w_down,
    ln_gain,
):
    owners = lax.axis_size(("band", "patch"))
    latent_width = w_embed.shape[1]
    grid_lat = jax.nn.silu(jnp.dot(grid_feat, w_embed, preferred_element_type=jnp.float32)).astype(
        jnp.bfloat16
    )
    sender_rows = jnp.take(grid_lat, g2m_sender[0], axis=0)
    projected = jnp.dot(sender_rows, w_send, preferred_element_type=jnp.float32)
    pre_act = projected + g2m_weight[0][:, None] * edge_vec.astype(jnp.float32)[None, :]
    messages = jax.nn.silu(pre_act).astype(jnp.bfloat16)
    slot_count = messages.shape[0] // owners
    arrived = lax.all_to_all(
        messages.reshape(owners, slot_count, latent_width),
        ("band", "patch"),
        split_axis=0,
        concat_axis=0,
        tiled=True,
    )
    arrived = arrived.reshape(owners * slot_count, latent_width)
    targets = g2m_target[0]
    mesh_rows = mesh_src.shape[0]
    block_rows = min(512, mesh_rows)
    row_ids = jnp.arange(mesh_rows, dtype=jnp.int32).reshape(mesh_rows // block_rows, block_rows)

    def sum_block(block_ids):
        onehot = (targets[None, :] == block_ids[:, None]).astype(jnp.bfloat16)
        return jnp.dot(onehot, arrived, preferred_element_type=jnp.float32)

    summed = lax.map(sum_block, row_ids).reshape(mesh_rows, latent_width).astype(jnp.bfloat16)
    mesh_h = jax.nn.silu(jnp.dot(summed, w_agg, preferred_element_type=jnp.float32)).astype(
        jnp.bfloat16
    )
    sources_first = jnp.transpose(mesh_src)
    for section_index in range(w_src.shape[0]):
        picked = jnp.take(mesh_h, halo_rows[0].reshape(-1), axis=0).reshape(4, -1, latent_width)
        from_low = patch_rim(picked[0], 1)
        from_high = patch_rim(picked[1], -1)
        from_south = band_rim(picked[2], 1)
        from_north = band_rim(picked[3], -1)
        extended = jnp.concatenate([mesh_h, from_low, from_high, from_south, from_north], axis=0)
        mesh_h = node_update(
            extended,
            mesh_h,
            sources_first,
            w_src[section_index],
            w_dst[section_index],
            w_up[section_index],
            w_down[section_index],
            ln_gain[section_index],
        )
    return mesh_h


def solution(mesh):
    return jax.shard_map(
        on_device,
        mesh=mesh,
        in_specs=(
            P(("band", "patch"), None),
            P(),
            P(),
            P(),
            P(("band", "patch"), None),
            P(("band", "patch"), None),
            P(("band", "patch"), None),
            P(),
            P(("band", "patch"), None, None),
            P(("band", "patch"), None),
            P(),
            P(),
            P(),
            P(),
            P(),
        ),
        out_specs=P(("band", "patch"), None),
        check_vma=False,
    )
```

profile of v0, /device:TPU:2, one launch (start us, length us, event | category | flops | bytes accessed | tf_op | source)
XLA Modules:
  0.0 237.2 jit_solution(15946204338552530381)
XLA Ops:
  2.2 2.3 multiply_convert_fusion.1
  4.6 17.3 %gather_fusion = bf16[4096,512]{1,0:T(8,128)(2,1)} fusion(bf16[2048,512]{1,0:T(8,128)(2,1)S(1)} %multiply_convert_fusion.1, s32[4096]{0:T(1024)S(1)} %broadcast_clamp_fusion), kind=kCustom, calls=%fused_computation.4 | custom fusion | bytes 8404992 | tf_op jit(solution)/shard_map/jit(_take)/gather | solution.py:68
  21.8 6.9 %multiply_convert_fusion = bf16[4096,512]{1,0:T(8,128)(2,1)} fusion(bf16[512,512]{1,0:T(8,128)(2,1)S(1)} %copy-done.16, f32[512]{0:T(512)S(1)} %convert_element_type.44, f32[4096]{0:T(1024)S(1)} %bitcast.96, bf16[4096,512]{1,0:T(8,128)(2,1)} %gather_fusion, pred[4096]{0:T(1024)(128)(4,1)S(1)} %compare_and_fusion.1), kind=kOutput, calls=%fused_computation.14 | convolution fusion | flops 2164260864 | bytes 8935424 | tf_op jit(solution)/shard_map/dot_general | solution.py:69
  28.8 11.0 %all-to-all-start = ((bf16[128,32,512]{2,1,0:T(8,128)(2,1)}), bf16[128,32,512]{2,1,0:T(8,128)(2,1)}, u32[]{:S(2)}, u32[]{:S(2)}) async-start(bf16[128,32,512]{2,1,0:T(8,128)(2,1)} %bitcast.89), calls=%async_computation | async-start | bytes 8388608 | tf_op jit(solution)/shard_map/all_to_all | solution.py:73
  40.0 51.8 %all-to-all-done = bf16[128,32,512]{2,1,0:T(8,128)(2,1)} async-done(((bf16[128,32,512]{2,1,0:T(8,128)(2,1)}), bf16[128,32,512]{2,1,0:T(8,128)(2,1)}, u32[]{:S(2)}, u32[]{:S(2)}) %all-to-all-start) | async-done | bytes 4194336 | tf_op jit(solution)/shard_map/all_to_all | solution.py:73
  91.7 9.2 %while.10 = (s32[]{:T(128)}, bf16[2,512,512]{2,1,0:T(8,128)(2,1)S(1)}, s32[1,4096]{1,0:T(1,128)S(1)}, s32[2,512]{1,0:T(2,128)S(1)}, bf16[4096,512]{1,0:T(8,128)(2,1)}, /*index=5*/s32[]{:T(128)}) while((s32[]{:T(128)}, bf16[2,512,512]{2,1,0:T(8,128)(2,1)S(1)}, s32[1,4096]{1,0:T(1,128)S(1)}, s32[2,512]{1,0:T(2,128)S(1)}, ...), condition=%wide.region_1.2_spmd, body=%wide.region_0.1_spmd.sunk | while | flops 2149580800 | bytes 5265485 | solution.py:90
  91.8 4.6 %fusion.81 = bf16[2,512,512]{2,1,0:T(8,128)(2,1)S(1)} fusion(bf16[2,512,512]{2,1,0:T(8,128)(2,1)S(1)} %get-tuple-element.101, s32[]{:T(128)} %get-tuple-element.100, bf16[4096,512]{1,0:T(8,128)(2,1)} %get-tuple-element.110, s32[4096]{0:T(1024)S(1)} %bitcast.97, s32[512]{0:T(512)S(1)} %bitcast.92), kind=kOutput, calls=%fused_computation.10.clone.1 | convolution fusion | flops 2149580800 | bytes 5261316 | tf_op jit(solution)/shard_map/while/body/eval_jaxpr/dot_general | solution.py:88
  96.4 4.6 %fusion.81 = bf16[2,512,512]{2,1,0:T(8,128)(2,1)S(1)} fusion(bf16[2,512,512]{2,1,0:T(8,128)(2,1)S(1)} %get-tuple-element.101, s32[]{:T(128)} %get-tuple-element.100, bf16[4096,512]{1,0:T(8,128)(2,1)} %get-tuple-element.110, s32[4096]{0:T(1024)S(1)} %bitcast.97, s32[512]{0:T(512)S(1)} %bitcast.92), kind=kOutput, calls=%fused_computation.10.clone.1 | convolution fusion | flops 2149580800 | bytes 5261316 | tf_op jit(solution)/shard_map/while/body/eval_jaxpr/dot_general | solution.py:88
  102.0 2.2 constant_dynamic-update-slice_fusion.4
  104.2 2.0 gather_fusion.1
  107.3 2.4 %collective-permute-start.1 = (bf16[128,512]{1,0:T(8,128)(2,1)S(1)}, bf16[128,512]{1,0:T(8,128)(2,1)S(1)}, u32[]{:S(2)}, u32[]{:S(2)}) collective-permute-start(bf16[128,512]{1,0:T(8,128)(2,1)S(1)} %get-tuple-element.55), channel_id=1, source_target_pairs={{0,3},{1,0},{2,1},{3,2},{4,7},{5,4},{6,5},{7,6},{8,11},{9,8},{10,9... | collective-permute-start | bytes 393224 | tf_op jit(solution)/shard_map/ppermute | solution.py:9
  109.7 1.9 collective-permute-start.2
  111.6 5.9 %collective-permute-start.3 = (bf16[128,512]{1,0:T(8,128)(2,1)S(1)}, bf16[128,512]{1,0:T(8,128)(2,1)S(1)}, u32[]{:S(2)}, u32[]{:S(2)}) collective-permute-start(bf16[128,512]{1,0:T(8,128)(2,1)S(1)} %get-tuple-element.53), channel_id=1, source_target_pairs={{4,0},{8,4},{12,8},{16,12},{20,16},{24,20},{28,24},{32,28},{36,32}... | collective-permute-start | bytes 393224 | tf_op jit(solution)/shard_map/ppermute | solution.py:15
  117.5 2.1 fusion.32
  119.6 3.1 %fusion.35 = f32[1024,512]{1,0:T(8,128)} fusion(bf16[1024,512]{1,0:T(8,128)(2,1)S(1)} %get-tuple-element.48, bf16[2,1024,512]{2,1,0:T(8,128)(2,1)} %param.33), kind=kOutput, calls=%fused_computation.46 | convolution fusion | flops 536870912 | bytes 3670016 | tf_op jit(solution)/shard_map/dot_general | solution.py:36
  122.9 25.4 %gather_fusion.2 = bf16[6144,512]{1,0:T(8,128)(2,1)} fusion(bf16[1536,512]{1,0:T(8,128)(2,1)S(1)} %constant_dynamic-update-slice_fusion, s32[6144]{0:T(1024)S(1)} %fusion.49), kind=kCustom, calls=%fused_computation.1.clone | custom fusion | bytes 12607488 | tf_op jit(solution)/shard_map/jit(_take)/gather | solution.py:29
  148.3 4.2 %broadcast_select_fusion.1 = bf16[6144,512]{1,0:T(8,128)(2,1)S(1)} fusion(bf16[6144,512]{1,0:T(8,128)(2,1)} %gather_fusion.2, pred[6144]{0:T(1024)(128)(4,1)S(1)} %compare_and_fusion), kind=kLoop, calls=%fused_computation.16 | loop fusion | flops 3145728 | bytes 12589056 | tf_op jit(solution)/shard_map/jit(_take)/select_n | solution.py:29
  152.5 5.6 %multiply_reduce_fusion.1 = bf16[1024,512]{1,0:T(8,128)(2,1)} fusion(f32[1024,512]{1,0:T(8,128)S(1)} %copy-done.8, bf16[6,1024,512]{2,1,0:T(8,128)(2,1)S(1)} %bitcast.88, bf16[2,512,512]{2,1,0:T(8,128)(2,1)S(1)} %copy-done.13), kind=kOutput, calls=%fused_computation.13 | convolution fusion | flops 3239575552 | bytes 9961472 | tf_op jit(solution)/shard_map/dot_general | solution.py:30
  158.1 4.4 %fusion.56 = (f32[1024]{0:T(1024)S(1)}, f32[1024,512]{0,1:T(8,128)}) fusion(bf16[2,512,512]{2,1,0:T(8,128)(2,1)} %param.34, f32[1024,512]{1,0:T(8,128)S(1)} %copy-done.7, bf16[1024,512]{1,0:T(8,128)(2,1)} %multiply_reduce_fusion.1, bf16[2,1024,512]{2,1,0:T(8,128)(2,1)} %param.33), kind=kOutput, calls=%fused_computation.91 | convolution fusion | flops 1077410816 | bytes 6295552 | tf_op jit(solution)/shard_map/dot_general | solution.py:39
  162.5 1.9 copy.18
  166.4 2.1 constant_dynamic-update-slice_fusion.9
  168.5 2.0 gather_fusion.3
  170.5 3.1 %fusion.24 = f32[1024,512]{1,0:T(8,128)} fusion(bf16[1024,512]{1,0:T(8,128)(2,1)S(1)} %get-tuple-element.46, bf16[2,512,512]{2,1,0:T(8,128)(2,1)} %param.32), kind=kOutput, calls=%fused_computation.36 | convolution fusion | flops 536870912 | bytes 3670016 | tf_op jit(solution)/shard_map/dot_general | solution.py:33
  173.9 3.2 %collective-permute-start.5 = (bf16[128,512]{1,0:T(8,128)(2,1)S(1)}, bf16[128,512]{1,0:T(8,128)(2,1)S(1)}, u32[]{:S(2)}, u32[]{:S(2)}) collective-permute-start(bf16[128,512]{1,0:T(8,128)(2,1)S(1)} %get-tuple-element.51), channel_id=1, source_target_pairs={{0,3},{1,0},{2,1},{3,2},{4,7},{5,4},{6,5},{7,6},{8,11},{9,8},{10,9... | collective-permute-start | bytes 393224 | tf_op jit(solution)/shard_map/ppermute | solution.py:9
  177.1 3.1 %fusion.27 = f32[1024,512]{1,0:T(8,128)} fusion(bf16[1024,512]{1,0:T(8,128)(2,1)S(1)} %get-tuple-element.46, bf16[2,1024,512]{2,1,0:T(8,128)(2,1)} %param.33), kind=kOutput, calls=%fused_computation.39 | convolution fusion | flops 536870912 | bytes 3670016 | tf_op jit(solution)/shard_map/dot_general | solution.py:36
  182.1 6.0 %collective-permute-start.7 = (bf16[128,512]{1,0:T(8,128)(2,1)S(1)}, bf16[128,512]{1,0:T(8,128)(2,1)S(1)}, u32[]{:S(2)}, u32[]{:S(2)}) collective-permute-start(bf16[128,512]{1,0:T(8,128)(2,1)S(1)} %get-tuple-element.49), channel_id=1, source_target_pairs={{4,0},{8,4},{12,8},{16,12},{20,16},{24,20},{28,24},{32,28},{36,32}... | collective-permute-start | bytes 393224 | tf_op jit(solution)/shard_map/ppermute | solution.py:15
  190.4 25.4 %gather_fusion.4 = bf16[6144,512]{1,0:T(8,128)(2,1)} fusion(bf16[1536,512]{1,0:T(8,128)(2,1)S(1)} %constant_dynamic-update-slice_fusion.5, s32[6144]{0:T(1024)S(1)} %fusion.49), kind=kCustom, calls=%fused_computation.3.clone | custom fusion | bytes 12607488 | tf_op jit(solution)/shard_map/jit(_take)/gather | solution.py:29
  215.8 4.2 %broadcast_select_fusion = bf16[6144,512]{1,0:T(8,128)(2,1)S(1)} fusion(bf16[6144,512]{1,0:T(8,128)(2,1)} %gather_fusion.4, pred[6144]{0:T(1024)(128)(4,1)S(1)} %compare_and_fusion), kind=kLoop, calls=%fused_computation.15 | loop fusion | flops 3145728 | bytes 12589056 | tf_op jit(solution)/shard_map/jit(_take)/select_n | solution.py:29
  220.1 5.6 %multiply_reduce_fusion = bf16[1024,512]{1,0:T(8,128)(2,1)} fusion(f32[1024,512]{1,0:T(8,128)S(1)} %copy-done.6, bf16[6,1024,512]{2,1,0:T(8,128)(2,1)S(1)} %bitcast.87, bf16[2,512,512]{2,1,0:T(8,128)(2,1)S(1)} %copy-done.14), kind=kOutput, calls=%fused_computation.12 | convolution fusion | flops 3239575552 | bytes 9961472 | tf_op jit(solution)/shard_map/dot_general | solution.py:30
  225.7 4.9 %fusion.59 = (f32[1024]{0:T(1024)S(1)}, f32[1024,512]{0,1:T(8,128)}) fusion(bf16[2,512,512]{2,1,0:T(8,128)(2,1)S(1)} %copy-done.15, f32[1024,512]{1,0:T(8,128)} %fusion.27, bf16[1024,512]{1,0:T(8,128)(2,1)} %multiply_reduce_fusion, bf16[2,1024,512]{2,1,0:T(8,128)(2,1)} %param.33), kind=kOutput, calls=%fused_computation.92 | convolution fusion | flops 1077410816 | bytes 6295552 | tf_op jit(solution)/shard_map/dot_general | solution.py:39
  230.6 2.9 %copy.19 = f32[1024,512]{1,0:T(8,128)} copy(f32[1024,512]{0,1:T(8,128)} %get-tuple-element.62) | data formatting | bytes 4194304 | tf_op jit(solution)/shard_map/dot_general | solution.py:39
  233.5 2.1 multiply_reduce_fusion.2
  (86 shorter events, 12.4 us)
Async XLA Ops:
  0.0 2.2 copy-start
  4.5 17.3 %copy-start.16 = (bf16[512,512]{1,0:T(8,128)(2,1)S(1)}, bf16[512,512]{1,0:T(8,128)(2,1)}, u32[]{:S(2)}) copy-start(bf16[512,512]{1,0:T(8,128)(2,1)} %param.23) | copy-start | bytes 1572868
  4.6 17.3 %copy-start.18 = (f32[1,4096]{1,0:T(1,128)S(1)}, f32[1,4096]{1,0:T(1,128)}, u32[]{:S(2)}) copy-start(f32[1,4096]{1,0:T(1,128)} %param.26) | copy-start | bytes 49156
  28.8 11.0 %copy-start.10 = (s32[1024,6]{0,1:T(8,128)S(1)}, s32[1024,6]{0,1:T(8,128)}, u32[]{:S(2)}) copy-start(s32[1024,6]{0,1:T(8,128)} %param.30) | copy-start | bytes 73732
  28.8 11.1 %copy-start.11 = (s32[1,4,128]{2,1,0:T(4,128)S(1)}, s32[1,4,128]{2,1,0:T(4,128)}, u32[]{:S(2)}) copy-start(s32[1,4,128]{2,1,0:T(4,128)} %param.29) | copy-start | bytes 6148
  28.8 11.1 %copy-start.12 = (f32[2,512]{1,0:T(2,128)S(1)}, f32[2,512]{1,0:T(2,128)}, u32[]{:S(2)}) copy-start(f32[2,512]{1,0:T(2,128)} %param.35) | copy-start | bytes 12292
  28.8 63.0 %copy-start.19 = (s32[1,4096]{1,0:T(1,128)S(1)}, s32[1,4096]{1,0:T(1,128)}, u32[]{:S(2)}) copy-start(s32[1,4096]{1,0:T(1,128)} %param.27) | copy-start | bytes 49156
  28.8 62.9 %all-to-all-start = ((bf16[128,32,512]{2,1,0:T(8,128)(2,1)}), bf16[128,32,512]{2,1,0:T(8,128)(2,1)}, u32[]{:S(2)}, u32[]{:S(2)}) async-start(bf16[128,32,512]{2,1,0:T(8,128)(2,1)} %bitcast.89), calls=%async_computation | async-start | bytes 8388608 | tf_op jit(solution)/shard_map/all_to_all | solution.py:73
  91.7 10.2 %copy-start.17 = (bf16[512,512]{1,0:T(8,128)(2,1)S(1)}, bf16[512,512]{1,0:T(8,128)(2,1)}, u32[]{:S(2)}) copy-start(bf16[512,512]{1,0:T(8,128)(2,1)} %param.28) | copy-start | bytes 1572868
  101.0 1.0 copy-start.20
  104.2 15.5 %copy-start.2 = (bf16[1024,512]{1,0:T(8,128)(2,1)}, bf16[1024,512]{1,0:T(8,128)(2,1)S(1)}, u32[]{:S(2)}) copy-start(bf16[1024,512]{1,0:T(8,128)(2,1)S(1)} %get-tuple-element.48) | copy-start | bytes 3145732
  106.2 11.4 %copy-start.9 = (bf16[2,512,512]{2,1,0:T(8,128)(2,1)S(1)}, bf16[2,512,512]{2,1,0:T(8,128)(2,1)}, u32[]{:S(2)}) copy-start(bf16[2,512,512]{2,1,0:T(8,128)(2,1)} %param.32) | copy-start | bytes 3145732
  106.4 16.4 %collective-permute-start = (bf16[128,512]{1,0:T(8,128)(2,1)S(1)}, bf16[128,512]{1,0:T(8,128)(2,1)S(1)}, u32[]{:S(2)}, u32[]{:S(2)}) collective-permute-start(bf16[128,512]{1,0:T(8,128)(2,1)S(1)} %get-tuple-element.56), channel_id=1, source_target_pairs={{0,1},{1,2},{2,3},{3,0},{4,5},{5,6},{6,7},{7,4},{8,9},{9,10},{10,1... | collective-permute-start | bytes 393224 | tf_op jit(solution)/shard_map/ppermute | solution.py:9
  107.3 15.5 %collective-permute-start.1 = (bf16[128,512]{1,0:T(8,128)(2,1)S(1)}, bf16[128,512]{1,0:T(8,128)(2,1)S(1)}, u32[]{:S(2)}, u32[]{:S(2)}) collective-permute-start(bf16[128,512]{1,0:T(8,128)(2,1)S(1)} %get-tuple-element.55), channel_id=1, source_target_pairs={{0,3},{1,0},{2,1},{3,2},{4,7},{5,4},{6,5},{7,6},{8,11},{9,8},{10,9... | collective-permute-start | bytes 393224 | tf_op jit(solution)/shard_map/ppermute | solution.py:9
  109.7 13.1 %collective-permute-start.2 = (bf16[128,512]{1,0:T(8,128)(2,1)S(1)}, bf16[128,512]{1,0:T(8,128)(2,1)S(1)}, u32[]{:S(2)}, u32[]{:S(2)}) collective-permute-start(bf16[128,512]{1,0:T(8,128)(2,1)S(1)} %get-tuple-element.54), channel_id=1, source_target_pairs={{0,4},{4,8},{8,12},{12,16},{16,20},{20,24},{24,28},{28,32},{32,36}... | collective-permute-start | bytes 393224 | tf_op jit(solution)/shard_map/ppermute | solution.py:15
  111.6 11.2 %collective-permute-start.3 = (bf16[128,512]{1,0:T(8,128)(2,1)S(1)}, bf16[128,512]{1,0:T(8,128)(2,1)S(1)}, u32[]{:S(2)}, u32[]{:S(2)}) collective-permute-start(bf16[128,512]{1,0:T(8,128)(2,1)S(1)} %get-tuple-element.53), channel_id=1, source_target_pairs={{4,0},{8,4},{12,8},{16,12},{20,16},{24,20},{28,24},{32,28},{36,32}... | collective-permute-start | bytes 393224 | tf_op jit(solution)/shard_map/ppermute | solution.py:15
  148.3 4.2 %copy-start.8 = (f32[1024,512]{1,0:T(8,128)S(1)}, f32[1024,512]{1,0:T(8,128)}, u32[]{:S(2)}) copy-start(f32[1024,512]{1,0:T(8,128)} %fusion.32) | copy-start | bytes 6291460
  148.3 4.2 %copy-start.13 = (bf16[2,512,512]{2,1,0:T(8,128)(2,1)S(1)}, bf16[2,512,512]{2,1,0:T(8,128)(2,1)}, u32[]{:S(2)}) copy-start(bf16[2,512,512]{2,1,0:T(8,128)(2,1)} %param.31) | copy-start | bytes 3145732
  152.5 5.6 %copy-start.7 = (f32[1024,512]{1,0:T(8,128)S(1)}, f32[1024,512]{1,0:T(8,128)}, u32[]{:S(2)}) copy-start(f32[1024,512]{1,0:T(8,128)} %fusion.35) | copy-start | bytes 6291460
  164.4 1.3 copy-start.4
  164.4 2.0 copy-start.3
  173.8 14.3 %collective-permute-start.4 = (bf16[128,512]{1,0:T(8,128)(2,1)S(1)}, bf16[128,512]{1,0:T(8,128)(2,1)S(1)}, u32[]{:S(2)}, u32[]{:S(2)}) collective-permute-start(bf16[128,512]{1,0:T(8,128)(2,1)S(1)} %get-tuple-element.52), channel_id=1, source_target_pairs={{0,1},{1,2},{2,3},{3,0},{4,5},{5,6},{6,7},{7,4},{8,9},{9,10},{10,1... | collective-permute-start | bytes 393224 | tf_op jit(solution)/shard_map/ppermute | solution.py:9
  173.9 14.3 %collective-permute-start.5 = (bf16[128,512]{1,0:T(8,128)(2,1)S(1)}, bf16[128,512]{1,0:T(8,128)(2,1)S(1)}, u32[]{:S(2)}, u32[]{:S(2)}) collective-permute-start(bf16[128,512]{1,0:T(8,128)(2,1)S(1)} %get-tuple-element.51), channel_id=1, source_target_pairs={{0,3},{1,0},{2,1},{3,2},{4,7},{5,4},{6,5},{7,6},{8,11},{9,8},{10,9... | collective-permute-start | bytes 393224 | tf_op jit(solution)/shard_map/ppermute | solution.py:9
  180.2 8.4 %collective-permute-start.6 = (bf16[128,512]{1,0:T(8,128)(2,1)S(1)}, bf16[128,512]{1,0:T(8,128)(2,1)S(1)}, u32[]{:S(2)}, u32[]{:S(2)}) collective-permute-start(bf16[128,512]{1,0:T(8,128)(2,1)S(1)} %get-tuple-element.50), channel_id=1, source_target_pairs={{0,4},{4,8},{8,12},{12,16},{16,20},{20,24},{24,28},{28,32},{32,36}... | collective-permute-start | bytes 393224 | tf_op jit(solution)/shard_map/ppermute | solution.py:15
  182.1 8.3 %collective-permute-start.7 = (bf16[128,512]{1,0:T(8,128)(2,1)S(1)}, bf16[128,512]{1,0:T(8,128)(2,1)S(1)}, u32[]{:S(2)}, u32[]{:S(2)}) collective-permute-start(bf16[128,512]{1,0:T(8,128)(2,1)S(1)} %get-tuple-element.49), channel_id=1, source_target_pairs={{4,0},{8,4},{12,8},{16,12},{20,16},{24,20},{28,24},{32,28},{36,32}... | collective-permute-start | bytes 393224 | tf_op jit(solution)/shard_map/ppermute | solution.py:15
  215.8 4.2 %copy-start.6 = (f32[1024,512]{1,0:T(8,128)S(1)}, f32[1024,512]{1,0:T(8,128)}, u32[]{:S(2)}) copy-start(f32[1024,512]{1,0:T(8,128)} %fusion.24) | copy-start | bytes 6291460
  215.8 4.2 %copy-start.14 = (bf16[2,512,512]{2,1,0:T(8,128)(2,1)S(1)}, bf16[2,512,512]{2,1,0:T(8,128)(2,1)}, u32[]{:S(2)}) copy-start(bf16[2,512,512]{2,1,0:T(8,128)(2,1)} %param.31) | copy-start | bytes 3145732
  220.1 5.6 %copy-start.15 = (bf16[2,512,512]{2,1,0:T(8,128)(2,1)S(1)}, bf16[2,512,512]{2,1,0:T(8,128)(2,1)}, u32[]{:S(2)}) copy-start(bf16[2,512,512]{2,1,0:T(8,128)(2,1)} %param.34) | copy-start | bytes 3145732
  233.5 2.2 copy-start.5
  235.7 1.5 copy-start.1
where the time goes:
time: 240 us; the launch traced here: 237 us
  local copies, waits for them, and re-layouts  79.7 us (33%)
  waiting for transfers between devices  54 us (22%)
  matrix products  52.5 us (22%)
  starting transfers between devices  33.3 us (14%)
  other arithmetic  17 us (7%)
    all_to_all x1, waiting for transfers between devices, on_device(): lax.all_to_all(messages.reshape(owners, slot_count, latent_width), ('band...  51.8 us
    gather x2, local copies, waits for them, and re-layouts, node_update(): chosen_rows = jnp.take(extended, sources_first.reshape(-1), axis=0)  50.8 us
    gather x1, local copies, waits for them, and re-layouts, on_device(): sender_rows = jnp.take(grid_lat, g2m_sender[0], axis=0)  17.3 us
    ppermute x4, starting transfers between devices, passed_along_2(): return lax.ppermute(x, axis, pairs)  15.7 us
    dot_general x2, matrix products, node_update(): jnp.dot(chosen_rows, w_src_l, preferred_element_type=jnp.float32)  11.2 us
    all_to_all x1, starting transfers between devices, on_device(): lax.all_to_all(messages.reshape(owners, slot_count, latent_width), ('band...  11 us
    dot_general x2, matrix products, node_update(): mixed = jnp.dot(hidden, w_down_l, preferred_element_type=jnp.float32)  9.32 us
    dot_general x2, matrix products, sum_block(): return jnp.dot(onehot, arrived, preferred_element_type=jnp.float32)  9.17 us
  transfers between devices with their start and end apart: 9, of which 3 were waited for; matrix products, arithmetic and copies ran while one was open for 4% of the time, Pallas kernels for 0%

commit v1 on v0

v1 whole, which is shorter than its diff:
```python
import jax
import jax.numpy as jnp
from jax import lax
from jax.experimental import pallas as pl
from jax.experimental.pallas import tpu as pltpu
from jax.sharding import PartitionSpec as P

MESH = pl.DeviceIdType.MESH
BF16 = jnp.bfloat16
F32 = jnp.float32
VARS, D, W = 227, 512, 256
GRID, M, SLOTS, OWNERS = 2048, 1024, 32, 128
HALO, DEG, LAYERS = 128, 6, 2
TILE = 128
CHUNK = 256
PAIRS = 16


def dot(a, b):
    return jnp.dot(a, b, preferred_element_type=F32)


def half_silu(h):
    return h + h * jnp.tanh(h)


def column(row):
    return jnp.transpose(jnp.broadcast_to(row, (TILE, TILE)))


def lanes(shape):
    return lax.broadcasted_iota(jnp.int32, shape, len(shape) - 1)


def put_rows(ref, at, value):
    rows = value.shape[0]
    for j in range(D // TILE):
        ref[pl.ds(at + j, rows, stride=4), :] = value[:, j * TILE : (j + 1) * TILE]


def kernel(
    feat_hbm, embed_hbm, send_hbm, vec_hbm, sender_hbm, length_hbm, target_hbm, agg_hbm, halo_hbm, src_hbm,
    wsrc_hbm, wdst_hbm, wup_hbm, wdown_hbm, gain_hbm,
    out_hbm,
    feat, embed, wsend, vec, sender, length, target, wagg, halo_ids, src, wsrc, wdst, wup, wdown, gain,
    feat_pad, wcat, pick, outbox, inbox, scatter, msgs, summed, ext, halo_pick, halo_out, halo_in,
    table, recv, sums, esum, up, src_v, src_s,
    in_sem, idx_sem, send_sem, recv_sem, halo_send, halo_recv, out_sem, ready,
):
    band, z = lax.axis_index("band"), lax.axis_index("patch")
    x, y, core = band // 8, (band // 2) % 4, band % 2
    me = band * 4 + z

    def loads():
        pairs = (
            (feat_hbm, feat), (sender_hbm, sender), (length_hbm, length), (embed_hbm, embed), (vec_hbm, vec),
            (target_hbm, target), (src_hbm, src), (halo_hbm, halo_ids), (send_hbm, wsend), (agg_hbm, wagg),
            (wsrc_hbm, wsrc), (wdst_hbm, wdst), (wup_hbm, wup), (wdown_hbm, wdown), (gain_hbm, gain),
        )
        return [pltpu.make_async_copy(a, b, in_sem.at[i]) for i, (a, b) in enumerate(pairs)]

    copies = loads()
    for copy in copies:
        copy.start()

    plane = [((((x + i) % 4) * 4 + (y + j) % 4) * 2 + core, z) for i in range(4) for j in range(4) if i or j]
    line = [(band // 2 * 2 + (core + i) % 2, (z + j) % 4) for i in range(2) for j in range(4) if i or j]
    barrier = pltpu.get_barrier_semaphore()
    for device in plane + line:
        pl.semaphore_signal(barrier, inc=1, device_id=device, device_id_type=MESH)

    feat_pad[W - 32 : W, :] = jnp.zeros((32, GRID), BF16)
    for i in (0, 1, 2):
        copies[i].wait()
    feat_pad[0:VARS, :] = feat[...]

    def pick_window(w):
        def band_of(i, j):
            return ((x + i) % 4 * 4 + (y + i + w) % 4) * 2 + (core + j) % 2

        for i in range(4):
            for j in range(2):
                ids = column(sender[pl.ds(band_of(i, j), 1), :])
                rows = slice((i * 2 + j) * TILE, (i * 2 + j + 1) * TILE)
                for k in range(GRID // TILE):
                    hit = ids == lanes((TILE, TILE)) + k * TILE
                    pick[rows, k * TILE : (k + 1) * TILE] = hit.astype(F32).astype(BF16)

    def rows_window(w):
        for i in range(4):
            both = lax.dot_general(
                pick[i * 2 * TILE : (i + 1) * 2 * TILE, :], feat_pad[...], (((1,), (1,)), ((), ())),
                preferred_element_type=F32,
            )
            for j in range(2):
                to = ((x + i) % 4 * 4 + (y + i + w) % 4) * 2 + (core + j) % 2
                rows = both[j * TILE : (j + 1) * TILE, :]
                long = column(length[pl.ds(to, 1), :])
                first = long.astype(BF16).astype(F32)
                second = (long - first).astype(BF16).astype(F32)
                third = long - first - second
                lane = lanes((TILE, TILE)) + TILE
                tail = rows[:, TILE:]
                tail = jnp.where(lane == VARS, first, tail)
                tail = jnp.where(lane == VARS + 1, second, tail)
                tail = jnp.where(lane == VARS + 2, third, tail)
                outbox[to, :, 0:TILE] = rows[:, :TILE].astype(BF16)
                outbox[to, :, TILE:W] = tail.astype(BF16)

    def send_window(w):
        for dz in range(4):
            for i in range(4):
                for j in range(2):
                    to = ((x + i) % 4 * 4 + (y + i + w) % 4) * 2 + (core + j) % 2
                    to_z = (z + dz) % 4
                    part = outbox.at[to, pl.ds(pl.multiple_of(to_z * SLOTS, SLOTS), SLOTS)]

                    def remote():
                        pltpu.make_async_remote_copy(
                            src_ref=part, dst_ref=inbox.at[me], send_sem=send_sem.at[0],
                            recv_sem=recv_sem.at[band // 2], device_id=(to, to_z), device_id_type=MESH,
                        ).start()

                    if i == 0 and j == 0 and dz == 0:
                        pl.when(w != 0)(remote)

                        @pl.when(w == 0)
                        def _():
                            pltpu.make_async_copy(part, inbox.at[me], recv_sem.at[band // 2]).start()
                    else:
                        remote()

    pick_window(0)
    pl.semaphore_wait(barrier, len(plane) + len(line))
    for device in line:
        pl.semaphore_signal(ready, inc=1, device_id=device, device_id_type=MESH)
    rows_window(0)
    pl.semaphore_wait(ready, len(line))
    send_window(0)

    @pl.loop(1, 4)
    def _(w):
        pick_window(w)
        rows_window(w)
        send_window(w)

    for copy in copies[3:]:
        copy.wait()
    wcat[...] = jnp.zeros((W, 2 * D), BF16)
    wcat[0:VARS, 0:D] = (embed[...].astype(F32) * 0.5).astype(BF16)
    edge_row = jnp.broadcast_to((vec[...].astype(F32) * 0.5).astype(BF16), (3, D))
    wcat[VARS : VARS + 3, D : 2 * D] = edge_row
    parity = (lanes((1, TILE)) + 1) % 2 * 4 + 4
    for k in range(DEG):
        for j in range(M // TILE):
            ids = src[k : k + 1, j * TILE : (j + 1) * TILE] * 4 + parity
            src_v[pl.ds(k * M + j * TILE, TILE)] = ids.reshape(TILE)
    src_copy = pltpu.make_async_copy(src_v, src_s, idx_sem)
    src_copy.start()
    for i in range(4):
        ids = column(halo_ids[i : i + 1, :])
        for k in range(M // TILE):
            hit = ids == lanes((TILE, TILE)) + k * TILE
            halo_pick[i * TILE : (i + 1) * TILE, k * TILE : (k + 1) * TILE] = hit.astype(F32).astype(BF16)
    summed[...] = jnp.zeros((M, D), F32)
    ends = (M + 4 * HALO) * 4 + 8
    table[0:8, :] = jnp.zeros((8, TILE), F32)
    table[ends : ends + 8, :] = jnp.zeros((8, TILE), F32)

    @pl.loop(0, 4)
    def _(w):
        def group(i):
            return (x + 4 - i) % 4 * 4 + (y + 8 - i - w) % 4

        for i in range(4):
            for h in range(2):
                ids = jnp.broadcast_to(target[pl.ds(group(i) * 2 + h, 1), :], (TILE, TILE))
                for k in range(M // TILE):
                    hit = ids == lax.broadcasted_iota(jnp.int32, (TILE, TILE), 0) + k * TILE
                    scatter[k * TILE : (k + 1) * TILE, (i * 2 + h) * TILE : (i * 2 + h + 1) * TILE] = hit.astype(
                        F32
                    ).astype(BF16)
        for i in range(4):
            g = group(i)
            part = inbox.at[pl.ds(pl.multiple_of(g * 8, 8), 8)]
            pltpu.make_async_copy(part, part, recv_sem.at[g]).wait()
            rows = inbox[pl.ds(pl.multiple_of(g * 8, 8), 8)].reshape(CHUNK, W)
            first = dot(rows, wcat[...])
            latent = half_silu(first[:, :D]).astype(BF16)
            pre = dot(latent, wsend[...]) * 0.5 + first[:, D:]
            msgs[i * CHUNK : (i + 1) * CHUNK, :] = half_silu(pre).astype(BF16)
        for k in range(M // CHUNK):
            rows = slice(k * CHUNK, (k + 1) * CHUNK)
            summed[rows, :] += dot(scatter[rows, :], msgs[...])

    for k in range(M // CHUNK):
        rows = slice(k * CHUNK, (k + 1) * CHUNK)
        ext[rows, :] = half_silu(dot(summed[rows, :].astype(BF16), wagg[...]) * 0.5).astype(BF16)
    src_copy.wait()

    neighbours = ((band, (z + 1) % 4), (band, (z + 3) % 4), ((band + 1) % 32, z), ((band + 31) % 32, z))
    low = lax.broadcasted_iota(jnp.int32, (8, TILE), 0) < 4

    @pl.loop(0, LAYERS)
    def _(layer):
        halos = []
        for i in range(4):
            rows = slice(i * HALO, (i + 1) * HALO)
            halo_out[layer, rows, :] = dot(halo_pick[rows, :], ext[...]).astype(BF16)
            copy = pltpu.make_async_remote_copy(
                src_ref=halo_out.at[layer, rows], dst_ref=halo_in.at[layer, rows],
                send_sem=halo_send.at[layer, i], recv_sem=halo_recv.at[layer, i],
                device_id=neighbours[i], device_id_type=MESH,
            )
            copy.start()
            halos.append(copy)
        for k in range(M // CHUNK):
            rows = slice(k * CHUNK, (k + 1) * CHUNK)
            own = ext[rows, :]
            put_rows(table, 8 + k * CHUNK * 4, dot(own, wsrc[layer]) * 0.5)
            put_rows(recv, k * CHUNK * 4, dot(own, wdst[layer]) * 0.5)
            up[rows, :] = dot(own, wup[layer, 0:D, :])
        for i in range(4):
            halos[i].wait()
            rows = slice(i * HALO, (i + 1) * HALO)
            value = dot(halo_in[layer, rows, :], wsrc[layer]) * 0.5
            if i == 2:
                value = jnp.where(band == 0, 0.0, value)
            if i == 3:
                value = jnp.where(band == 31, 0.0, value)
            put_rows(table, 8 + (M + i * HALO) * 4, value)

        @pl.loop(0, M // 2 // PAIRS)
        def _(t):
            for u in range(PAIRS):
                at = pl.ds(pl.multiple_of((t * PAIRS + u) * 8, 8), 8)
                here = recv[at, :]
                total = None
                for k in range(DEG):
                    a = src_s[t * (2 * PAIRS) + (k * M + 2 * u)]
                    b = src_s[t * (2 * PAIRS) + (k * M + 2 * u + 1)]
                    h = jnp.where(low, table[pl.ds(a, 8), :], table[pl.ds(b, 8), :]) + here
                    s = half_silu(h)
                    total = s if total is None else total + s
                sums[at, :] = total

        for k in range(M // CHUNK):
            rows = slice(k * CHUNK, (k + 1) * CHUNK)
            for j in range(D // TILE):
                esum[rows, j * TILE : (j + 1) * TILE] = sums[pl.ds(k * CHUNK * 4 + j, CHUNK, stride=4), :].astype(BF16)
            hidden = half_silu((up[rows, :] + dot(esum[rows, :], wup[layer, D : 2 * D, :])) * 0.5).astype(BF16)
            mixed = dot(hidden, wdown[layer])
            centre = mixed - jnp.mean(mixed, axis=1, keepdims=True)
            spread = jnp.mean(centre * centre, axis=1, keepdims=True)
            normed = centre * lax.rsqrt(spread + 1e-05) * gain[pl.ds(layer, 1), :]
            ext[rows, :] = (ext[rows, :].astype(F32) + normed).astype(BF16)

    result = pltpu.make_async_copy(ext, out_hbm, out_sem)
    result.start()
    result.wait()
    sent = inbox.at[pl.ds(0, OWNERS - 1)]
    pltpu.make_async_copy(sent, sent, send_sem.at[0]).wait()


def on_device(
    grid_feat, w_embed, w_send, edge_vec, g2m_sender, g2m_weight, g2m_target, w_agg, halo_rows, mesh_src,
    w_src, w_dst, w_up, w_down, ln_gain,
):
    args = (
        grid_feat.T, w_embed, w_send, edge_vec.reshape(1, D), g2m_sender.reshape(32, TILE), g2m_weight.reshape(32, TILE),
        g2m_target.reshape(32, TILE), w_agg, halo_rows.reshape(4, HALO), mesh_src.T, w_src, w_dst, w_up, w_down, ln_gain,
    )
    VM = pltpu.VMEM
    staged = [VM(a.shape, a.dtype) for a in args]
    scratch = [
        VM((W, GRID), BF16),
        VM((W, 2 * D), BF16),
        VM((8 * TILE, GRID), BF16),
        VM((32, TILE, W), BF16),
        VM((OWNERS, SLOTS, W), BF16),
        VM((M, 4 * CHUNK), BF16),
        VM((4 * CHUNK, D), BF16),
        VM((M, D), F32),
        VM((M, D), BF16),
        VM((4 * HALO, M), BF16),
        VM((LAYERS, 4 * HALO, D), BF16),
        VM((LAYERS, 4 * HALO, D), BF16),
        VM(((M + 4 * HALO) * 4 + 16, TILE), F32),
        VM((M * 4, TILE), F32),
        VM((M * 4, TILE), F32),
        VM((M, D), BF16),
        VM((M, D), F32),
        VM((DEG * M,), jnp.int32),
        pltpu.SMEM((DEG * M,), jnp.int32),
        pltpu.SemaphoreType.DMA((len(args),)),
        pltpu.SemaphoreType.DMA,
        pltpu.SemaphoreType.DMA((1,)),
        pltpu.SemaphoreType.DMA((16,)),
        pltpu.SemaphoreType.DMA((LAYERS, 4)),
        pltpu.SemaphoreType.DMA((LAYERS, 4)),
        pltpu.SemaphoreType.DMA,
        pltpu.SemaphoreType.REGULAR,
    ]
    anywhere = pl.BlockSpec(memory_space=pl.ANY)
    return pl.pallas_call(
        kernel,
        out_shape=jax.ShapeDtypeStruct((M, D), BF16),
        in_specs=[anywhere] * len(args),
        out_specs=anywhere,
        scratch_shapes=staged + scratch,
        compiler_params=pltpu.CompilerParams(collective_id=0, has_side_effects=True, vmem_limit_bytes=56 * 2**20),
    )(*args)


def solution(mesh):
    split = P(("band", "patch"), None)
    return jax.shard_map(
        on_device,
        mesh=mesh,
        in_specs=(
            split, P(), P(), P(), split, split, split, P(), P(("band", "patch"), None, None), split,
            P(), P(), P(), P(), P(),
        ),
        out_specs=split,
        check_vma=False,
    )
```

time: 240 us -> 77.7 us (0.32)
  local copies, waits for them, and re-layouts: 79.7 us -> 3.52 us
  Pallas kernels: 0 us -> 73.3 us
  waiting for transfers between devices: 54 us -> 0 us
  matrix products: 52.5 us -> 0 us
  starting transfers between devices: 33.3 us -> 0 us
  other arithmetic: 17 us -> 0 us
    pallas_call x0 -> x1, Pallas kernels: none -> 73.3 us  [on_device(): pl.pallas_call(kernel, out_shape=jax.ShapeDtypeStruct((M, D), BF16), in_s...]
    gather x5 -> x0, local copies, waits for them, and re-layouts: 72.1 us -> none  [the longest x2 50.8 us: node_update(): chosen_rows = jnp.take(extended, sources_first.reshape(-1), axis=0)]
    dot_general x13 -> x0, matrix products: 52.5 us -> none  [the longest x2 11.2 us: node_update(): jnp.dot(chosen_rows, w_src_l, preferred_element_type=jnp.float32)]
    all_to_all x1 -> x0, waiting for transfers between devices: 51.8 us -> none  [on_device(): lax.all_to_all(messages.reshape(owners, slot_count, latent_width), ('band...]
    ppermute x8 -> x0, starting transfers between devices: 22.3 us -> none  [the longest x4 15.7 us: passed_along_2(): return lax.ppermute(x, axis, pairs)]
    all_to_all x1 -> x0, starting transfers between devices: 11 us -> none  [on_device(): lax.all_to_all(messages.reshape(owners, slot_count, latent_width), ('band...]
    select_n x6 -> x0, other arithmetic: 9.54 us -> none  [the longest x2 8.45 us: node_update(): chosen_rows = jnp.take(extended, sources_first.reshape(-1), axis=0)]
    dot_general x2 -> x0, local copies, waits for them, and re-layouts: 4.81 us -> none  [node_update(): mixed = jnp.dot(hidden, w_down_l, preferred_element_type=jnp.float32)]
  transfers between devices with their start and end apart: 9 -> 0, of which waited for: 3 -> 0; matrix products, arithmetic and copies ran while one was open for 4% -> 0% of each run, Pallas kernels for 0% -> 0%
where the time goes in v1:
time: 77.7 us; the launch traced here: 76.8 us
  Pallas kernels  73.3 us (94%)
  local copies, waits for them, and re-layouts  3.52 us (5%)
    pallas_call x1, Pallas kernels, on_device(): pl.pallas_call(kernel, out_shape=jax.ShapeDtypeStruct((M, D), BF16), in_s...  73.3 us
    unnamed x1, local copies, waits for them, and re-layouts  2.26 us

profile of v1, /device:TPU:2, one launch (start us, length us, event | category | flops | bytes accessed | tf_op | source)
XLA Modules:
  0.0 76.8 jit_solution(2682894179124777758)
XLA Ops:
  0.0 1.3 %reshape.15.vec_hbm = bf16[1,512]{1,0:T(2,128)(2,1)} reshape(bf16[512]{0:T(512)(128)(2,1)} %param.18) | data formatting | bytes 2048 | tf_op jit(solution)/shard_map/reshape | solution.py:270
  1.3 73.3 %shard_map.145 = bf16[1024,512]{1,0:T(8,128)(2,1)} custom-call(bf16[227,2048]{1,0:T(8,128)(2,1)} %bitcast.6, bf16[227,512]{1,0:T(8,128)(2,1)} %embed_hbm.1, bf16[512,512]{1,0:T(8,128)(2,1)} %send_hbm.1, bf16[1,512]{1,0:T(2,128)(2,1)} %reshape.15.vec_hbm, s32[32,128]{1,0:T(8,128)} %bitcast.8, f32[32,128]{1,0:T(8,128)} %bitcast.9, s32[32,128]{1,0:T(8,128)} %bitcast.10, ...), custom_call_target="tpu_custom_call" | custom-call | tf_op jit(solution)/shard_map/pallas_call | solution.py:305
  74.6 2.3 %copy.17 = bf16[1024,512]{1,0:T(8,128)(2,1)} copy(bf16[1024,512]{1,0:T(8,128)(2,1)} %shard_map.145) | data formatting | bytes 2097152

commit v2 on v1

--- a/solution.py
+++ b/solution.py
@@ -43,25 +43,20 @@
     wsrc_hbm, wdst_hbm, wup_hbm, wdown_hbm, gain_hbm,
     out_hbm,
     feat, embed, wsend, vec, sender, length, target, wagg, halo_ids, src, wsrc, wdst, wup, wdown, gain,
-    feat_pad, wcat, pick, outbox, inbox, scatter, msgs, summed, ext, halo_pick, halo_out, halo_in,
+    feat_pad, wcat, pick, outbox, inbox, turned, scatter, msgs, summed, ext, halo_pick, halo_out, halo_in,
     table, recv, sums, esum, up, src_v, src_s,
     in_sem, idx_sem, send_sem, recv_sem, halo_send, halo_recv, out_sem, ready,
 ):
     band, z = lax.axis_index("band"), lax.axis_index("patch")
     x, y, core = band // 8, (band // 2) % 4, band % 2
-    me = band * 4 + z
 
     def loads():
         pairs = (
-            (feat_hbm, feat), (sender_hbm, sender), (length_hbm, length), (embed_hbm, embed), (vec_hbm, vec),
+            (sender_hbm, sender), (feat_hbm, feat), (length_hbm, length), (embed_hbm, embed), (vec_hbm, vec),
             (target_hbm, target), (src_hbm, src), (halo_hbm, halo_ids), (send_hbm, wsend), (agg_hbm, wagg),
             (wsrc_hbm, wsrc), (wdst_hbm, wdst), (wup_hbm, wup), (wdown_hbm, wdown), (gain_hbm, gain),
         )
         return [pltpu.make_async_copy(a, b, in_sem.at[i]) for i, (a, b) in enumerate(pairs)]
-
-    copies = loads()
-    for copy in copies:
-        copy.start()
 
     plane = [((((x + i) % 4) * 4 + (y + j) % 4) * 2 + core, z) for i in range(4) for j in range(4) if i or j]
     line = [(band // 2 * 2 + (core + i) % 2, (z + j) % 4) for i in range(2) for j in range(4) if i or j]
@@ -69,10 +64,9 @@
     for device in plane + line:
         pl.semaphore_signal(barrier, inc=1, device_id=device, device_id_type=MESH)
 
-    feat_pad[W - 32 : W, :] = jnp.zeros((32, GRID), BF16)
-    for i in (0, 1, 2):
-        copies[i].wait()
-    feat_pad[0:VARS, :] = feat[...]
+    copies = loads()
+    for copy in copies:
+        copy.start()
 
     def pick_window(w):
         def band_of(i, j):
@@ -117,8 +111,8 @@
 
                     def remote():
                         pltpu.make_async_remote_copy(
-                            src_ref=part, dst_ref=inbox.at[me], send_sem=send_sem.at[0],
-                            recv_sem=recv_sem.at[band // 2], device_id=(to, to_z), device_id_type=MESH,
+                            src_ref=part, dst_ref=inbox.at[w * 4 + dz, i * 2 + j], send_sem=send_sem.at[0],
+                            recv_sem=recv_sem.at[w * 4 + dz], device_id=(to, to_z), device_id_type=MESH,
                         ).start()
 
                     if i == 0 and j == 0 and dz == 0:
@@ -126,11 +120,16 @@
 
                         @pl.when(w == 0)
                         def _():
-                            pltpu.make_async_copy(part, inbox.at[me], recv_sem.at[band // 2]).start()
+                            pltpu.make_async_copy(part, inbox.at[0, 0], recv_sem.at[0]).start()
                     else:
                         remote()
 
+    copies[0].wait()
     pick_window(0)
+    feat_pad[W - 32 : W, :] = jnp.zeros((32, GRID), BF16)
+    copies[1].wait()
+    copies[2].wait()
+    feat_pad[0:VARS, :] = feat[...]
     pl.semaphore_wait(barrier, len(plane) + len(line))
     for device in line:
         pl.semaphore_signal(ready, inc=1, device_id=device, device_id_type=MESH)
@@ -148,7 +147,7 @@
         copy.wait()
     wcat[...] = jnp.zeros((W, 2 * D), BF16)
     wcat[0:VARS, 0:D] = (embed[...].astype(F32) * 0.5).astype(BF16)
-    edge_row = jnp.broadcast_to((vec[...].astype(F32) * 0.5).astype(BF16), (3, D))
+    edge_row = jnp.broadcast_to((vec[...].astype(F32) * 0.5)[None, :], (3, D)).astype(BF16)
     wcat[VARS : VARS + 3, D : 2 * D] = edge_row
     parity = (lanes((1, TILE)) + 1) % 2 * 4 + 4
     for k in range(DEG):
@@ -167,31 +166,51 @@
     table[0:8, :] = jnp.zeros((8, TILE), F32)
     table[ends : ends + 8, :] = jnp.zeros((8, TILE), F32)
 
-    @pl.loop(0, 4)
-    def _(w):
-        def group(i):
-            return (x + 4 - i) % 4 * 4 + (y + 8 - i - w) % 4
-
-        for i in range(4):
-            for h in range(2):
-                ids = jnp.broadcast_to(target[pl.ds(group(i) * 2 + h, 1), :], (TILE, TILE))
-                for k in range(M // TILE):
-                    hit = ids == lax.broadcasted_iota(jnp.int32, (TILE, TILE), 0) + k * TILE
-                    scatter[k * TILE : (k + 1) * TILE, (i * 2 + h) * TILE : (i * 2 + h + 1) * TILE] = hit.astype(
-                        F32
-                    ).astype(BF16)
-        for i in range(4):
-            g = group(i)
-            part = inbox.at[pl.ds(pl.multiple_of(g * 8, 8), 8)]
-            pltpu.make_async_copy(part, part, recv_sem.at[g]).wait()
-            rows = inbox[pl.ds(pl.multiple_of(g * 8, 8), 8)].reshape(CHUNK, W)
-            first = dot(rows, wcat[...])
-            latent = half_silu(first[:, :D]).astype(BF16)
-            pre = dot(latent, wsend[...]) * 0.5 + first[:, D:]
-            msgs[i * CHUNK : (i + 1) * CHUNK, :] = half_silu(pre).astype(BF16)
+    for q in range(4):
+        turned[q] = pltpu.roll(target[...], (4 - z + q) % 4 * SLOTS, 1)
+
+    def scatter_part(w, dz):
+        back = (4 - dz) % 4
+        block = lanes((1, TILE)) // SLOTS
+        for h in range(2):
+            ids = None
+            for p in range(4):
+                i, j = (h * 4 + p) // 2, p % 2
+                source = ((x + 4 - i) % 4 * 4 + (y + 8 - i - w) % 4) * 2 + (core + j) % 2
+                row = turned[(p - back) % 4, pl.ds(source, 1), :]
+                ids = row if ids is None else jnp.where(block == p, row, ids)
+            ids = jnp.broadcast_to(ids, (TILE, TILE))
+            at = dz * CHUNK + h * TILE
+            for k in range(M // TILE):
+                hit = ids == lax.broadcasted_iota(jnp.int32, (TILE, TILE), 0) + k * TILE
+                scatter[k * TILE : (k + 1) * TILE, at : at + TILE] = hit.astype(F32).astype(BF16)
+
+    def messages_part(w, dz):
+        part = inbox.at[w * 4 + dz]
+        pltpu.make_async_copy(part, part, recv_sem.at[w * 4 + dz]).wait()
+        first = dot(part[...].reshape(CHUNK, W), wcat[...])
+        latent = half_silu(first[:, :D]).astype(BF16)
+        pre = dot(latent, wsend[...]) * 0.5 + first[:, D:]
+        msgs[dz * CHUNK : (dz + 1) * CHUNK, :] = half_silu(pre).astype(BF16)
+
+    def add_parts(lo, hi):
         for k in range(M // CHUNK):
             rows = slice(k * CHUNK, (k + 1) * CHUNK)
-            summed[rows, :] += dot(scatter[rows, :], msgs[...])
+            summed[rows, :] += dot(scatter[rows, lo * CHUNK : hi * CHUNK], msgs[lo * CHUNK : hi * CHUNK, :])
+
+    @pl.loop(0, 3)
+    def _(w):
+        for dz in range(4):
+            scatter_part(w, dz)
+        for dz in range(4):
+            messages_part(w, dz)
+        add_parts(0, 4)
+
+    for dz in range(4):
+        scatter_part(3, dz)
+    for dz in range(4):
+        messages_part(3, dz)
+        add_parts(dz, dz + 1)
 
     for k in range(M // CHUNK):
         rows = slice(k * CHUNK, (k + 1) * CHUNK)
@@ -206,7 +225,9 @@
         halos = []
         for i in range(4):
             rows = slice(i * HALO, (i + 1) * HALO)
-            halo_out[layer, rows, :] = dot(halo_pick[rows, :], ext[...]).astype(BF16)
+            if i % 2 == 0:
+                both = slice(i * HALO, (i + 2) * HALO)
+                halo_out[layer, both, :] = dot(halo_pick[both, :], ext[...]).astype(BF16)
             copy = pltpu.make_async_remote_copy(
                 src_ref=halo_out.at[layer, rows], dst_ref=halo_in.at[layer, rows],
                 send_sem=halo_send.at[layer, i], recv_sem=halo_recv.at[layer, i],
@@ -237,8 +258,8 @@
                 here = recv[at, :]
                 total = None
                 for k in range(DEG):
-                    a = src_s[t * (2 * PAIRS) + (k * M + 2 * u)]
-                    b = src_s[t * (2 * PAIRS) + (k * M + 2 * u + 1)]
+                    a = src_s.at[pl.ds(k * M + 2 * u, M - 2 * PAIRS + 1)][t * (2 * PAIRS)]
+                    b = src_s.at[pl.ds(k * M + 2 * u + 1, M - 2 * PAIRS + 1)][t * (2 * PAIRS)]
                     h = jnp.where(low, table[pl.ds(a, 8), :], table[pl.ds(b, 8), :]) + here
                     s = half_silu(h)
                     total = s if total is None else total + s
@@ -258,7 +279,9 @@
     result = pltpu.make_async_copy(ext, out_hbm, out_sem)
     result.start()
     result.wait()
-    sent = inbox.at[pl.ds(0, OWNERS - 1)]
+    for s in range(15):
+        pltpu.make_async_copy(inbox.at[s], inbox.at[s], send_sem.at[0]).wait()
+    sent = inbox.at[15, pl.ds(0, 7)]
     pltpu.make_async_copy(sent, sent, send_sem.at[0]).wait()
 
 
@@ -267,7 +290,7 @@
     w_src, w_dst, w_up, w_down, ln_gain,
 ):
     args = (
-        grid_feat.T, w_embed, w_send, edge_vec.reshape(1, D), g2m_sender.reshape(32, TILE), g2m_weight.reshape(32, TILE),
+        grid_feat.T, w_embed, w_send, edge_vec, g2m_sender.reshape(32, TILE), g2m_weight.reshape(32, TILE),
         g2m_target.reshape(32, TILE), w_agg, halo_rows.reshape(4, HALO), mesh_src.T, w_src, w_dst, w_up, w_down, ln_gain,
     )
     VM = pltpu.VMEM
@@ -277,7 +300,8 @@
         VM((W, 2 * D), BF16),
         VM((8 * TILE, GRID), BF16),
         VM((32, TILE, W), BF16),
-        VM((OWNERS, SLOTS, W), BF16),
+        VM((16, 8, SLOTS, W), BF16),
+        VM((4, 32, TILE), jnp.int32),
         VM((M, 4 * CHUNK), BF16),
         VM((4 * CHUNK, D), BF16),
         VM((M, D), F32),

time: 77.7 us -> 72.6 us (0.934)
  Pallas kernels: 73.3 us -> 69.2 us
  local copies, waits for them, and re-layouts: 3.52 us -> 2.26 us
    pallas_call x1, Pallas kernels: 73.3 us -> 69.2 us  [on_device(): pl.pallas_call(kernel, out_shape=jax.ShapeDtypeStruct((M, D), BF16), in_s...]
    reshape x1 -> x0, local copies, waits for them, and re-layouts: 1.26 us -> none  [on_device(): edge_vec.reshape(1, D)]
where the time goes in v2:
time: 72.6 us; the launch traced here: 71.4 us
  Pallas kernels  69.2 us (95%)
  local copies, waits for them, and re-layouts  2.26 us (3%)
    pallas_call x1, Pallas kernels, on_device(): pl.pallas_call(kernel, out_shape=jax.ShapeDtypeStruct((M, D), BF16), in_s...  69.2 us
    unnamed x1, local copies, waits for them, and re-layouts  2.26 us

profile of v2, /device:TPU:2, one launch (start us, length us, event | category | flops | bytes accessed | tf_op | source)
XLA Modules:
  0.0 71.4 jit_solution(12794845889031607721)
XLA Ops:
  0.0 69.2 %shard_map.145 = bf16[1024,512]{1,0:T(8,128)(2,1)} custom-call(bf16[227,2048]{1,0:T(8,128)(2,1)} %bitcast.6, bf16[227,512]{1,0:T(8,128)(2,1)} %embed_hbm.1, bf16[512,512]{1,0:T(8,128)(2,1)} %send_hbm.1, bf16[512]{0:T(512)(128)(2,1)} %vec_hbm.1, s32[32,128]{1,0:T(8,128)} %bitcast.8, f32[32,128]{1,0:T(8,128)} %bitcast.9, s32[32,128]{1,0:T(8,128)} %bitcast.10, ...), custom_call_target="tpu_custom_call" | custom-call | tf_op jit(solution)/shard_map/pallas_call | solution.py:329
  69.2 2.3 %copy.17 = bf16[1024,512]{1,0:T(8,128)(2,1)} copy(bf16[1024,512]{1,0:T(8,128)(2,1)} %shard_map.145) | data formatting | bytes 2097152

commit v3 on v2

--- a/solution.py
+++ b/solution.py
@@ -9,11 +9,12 @@
 BF16 = jnp.bfloat16
 F32 = jnp.float32
 VARS, D, W = 227, 512, 256
-GRID, M, SLOTS, OWNERS = 2048, 1024, 32, 128
+GRID, M, SLOTS = 2048, 1024, 32
 HALO, DEG, LAYERS = 128, 6, 2
 TILE = 128
 CHUNK = 256
 PAIRS = 16
+AHEAD = 6
 
 
 def dot(a, b):
@@ -43,7 +44,7 @@
     wsrc_hbm, wdst_hbm, wup_hbm, wdown_hbm, gain_hbm,
     out_hbm,
     feat, embed, wsend, vec, sender, length, target, wagg, halo_ids, src, wsrc, wdst, wup, wdown, gain,
-    feat_pad, wcat, pick, outbox, inbox, turned, scatter, msgs, summed, ext, halo_pick, halo_out, halo_in,
+    feat_pad, wcat, pick, outbox, inbox, sender_turned, length_turned, target_turned, scatter, msgs, summed, ext, halo_pick, halo_out, halo_in,
     table, recv, sums, esum, up, src_v, src_s,
     in_sem, idx_sem, send_sem, recv_sem, halo_send, halo_recv, out_sem, ready,
 ):
@@ -68,80 +69,103 @@
     for copy in copies:
         copy.start()
 
-    def pick_window(w):
-        def band_of(i, j):
-            return ((x + i) % 4 * 4 + (y + i + w) % 4) * 2 + (core + j) % 2
-
-        for i in range(4):
-            for j in range(2):
-                ids = column(sender[pl.ds(band_of(i, j), 1), :])
-                rows = slice((i * 2 + j) * TILE, (i * 2 + j + 1) * TILE)
-                for k in range(GRID // TILE):
-                    hit = ids == lanes((TILE, TILE)) + k * TILE
-                    pick[rows, k * TILE : (k + 1) * TILE] = hit.astype(F32).astype(BF16)
-
-    def rows_window(w):
-        for i in range(4):
-            both = lax.dot_general(
-                pick[i * 2 * TILE : (i + 1) * 2 * TILE, :], feat_pad[...], (((1,), (1,)), ((), ())),
-                preferred_element_type=F32,
-            )
-            for j in range(2):
-                to = ((x + i) % 4 * 4 + (y + i + w) % 4) * 2 + (core + j) % 2
-                rows = both[j * TILE : (j + 1) * TILE, :]
-                long = column(length[pl.ds(to, 1), :])
-                first = long.astype(BF16).astype(F32)
-                second = (long - first).astype(BF16).astype(F32)
-                third = long - first - second
-                lane = lanes((TILE, TILE)) + TILE
-                tail = rows[:, TILE:]
-                tail = jnp.where(lane == VARS, first, tail)
-                tail = jnp.where(lane == VARS + 1, second, tail)
-                tail = jnp.where(lane == VARS + 2, third, tail)
-                outbox[to, :, 0:TILE] = rows[:, :TILE].astype(BF16)
-                outbox[to, :, TILE:W] = tail.astype(BF16)
-
-    def send_window(w):
-        for dz in range(4):
-            for i in range(4):
-                for j in range(2):
-                    to = ((x + i) % 4 * 4 + (y + i + w) % 4) * 2 + (core + j) % 2
-                    to_z = (z + dz) % 4
-                    part = outbox.at[to, pl.ds(pl.multiple_of(to_z * SLOTS, SLOTS), SLOTS)]
-
-                    def remote():
-                        pltpu.make_async_remote_copy(
-                            src_ref=part, dst_ref=inbox.at[w * 4 + dz, i * 2 + j], send_sem=send_sem.at[0],
-                            recv_sem=recv_sem.at[w * 4 + dz], device_id=(to, to_z), device_id_type=MESH,
-                        ).start()
-
-                    if i == 0 and j == 0 and dz == 0:
-                        pl.when(w != 0)(remote)
-
-                        @pl.when(w == 0)
-                        def _():
-                            pltpu.make_async_copy(part, inbox.at[0, 0], recv_sem.at[0]).start()
-                    else:
-                        remote()
-
-    copies[0].wait()
-    pick_window(0)
-    feat_pad[W - 32 : W, :] = jnp.zeros((32, GRID), BF16)
-    copies[1].wait()
-    copies[2].wait()
-    feat_pad[0:VARS, :] = feat[...]
+    block = lanes((1, TILE)) // SLOTS
+
+    def sign(piece, way):
+        return 1 - 2 * core if way == 1 else 2 * ((core + piece % 2) % 2) - 1
+
+    def band_at(part, piece, way):
+        i, j, w = piece // 2, piece % 2, part // 4
+        s = sign(piece, way)
+        return ((x + 4 + s * i) % 4 * 4 + (y + 8 + s * (i + w)) % 4) * 2 + (core + j) % 2
+
+    def z_at(part, piece, way):
+        return (z + 4 + sign(piece, way) * (part % 4)) % 4
+
+    def turn(ref, turned):
+        for q in range(4):
+            turned[q] = pltpu.roll(ref[...], (4 - z + q) % 4 * SLOTS, 1)
+
+    def pieces(turned, part, half, way):
+        row = None
+        for p in range(4):
+            got = turned[(p + 4 + z - z_at(part, p, way)) % 4, pl.ds(band_at(part, half * 4 + p, way), 1), :]
+            row = got if row is None else jnp.where(block == p, got, row)
+        return row
+
+    def gather_part(part):
+        for half in range(2):
+            ids = column(pieces(sender_turned, part, half, 1))
+            for k in range(GRID // TILE):
+                hit = ids == lanes((TILE, TILE)) + k * TILE
+                pick[half * TILE : (half + 1) * TILE, k * TILE : (k + 1) * TILE] = hit.astype(F32).astype(BF16)
+        both = lax.dot_general(
+            pick[...], feat_pad[...], (((1,), (1,)), ((), ())), preferred_element_type=F32
+        )
+        for half in range(2):
+            rows = both[half * TILE : (half + 1) * TILE, :]
+            long = column(pieces(length_turned, part, half, 1))
+            first = long.astype(BF16).astype(F32)
+            second = (long - first).astype(BF16).astype(F32)
+            third = long - first - second
+            lane = lanes((TILE, TILE)) + TILE
+            tail = rows[:, TILE:]
+            tail = jnp.where(lane == VARS, first, tail)
+            tail = jnp.where(lane == VARS + 1, second, tail)
+            tail = jnp.where(lane == VARS + 2, third, tail)
+            to = slice(half * TILE, (half + 1) * TILE)
+            outbox[part, to, 0:TILE] = rows[:, :TILE].astype(BF16)
+            outbox[part, to, TILE:W] = tail.astype(BF16)
+
+    def send_part(part):
+        to_z = z_at(part, 0, 1)
+        for piece in range(8):
+            rows = outbox.at[part, pl.ds(piece * SLOTS, SLOTS)]
+            there = inbox.at[part, pl.ds(piece * SLOTS, SLOTS)]
+
+            def remote():
+                pltpu.make_async_remote_copy(
+                    src_ref=rows, dst_ref=there, send_sem=send_sem.at[part], recv_sem=recv_sem.at[part],
+                    device_id=(band_at(part, piece, 1), to_z), device_id_type=MESH,
+                ).start()
+
+            if piece == 0:
+                pl.when(part != 0)(remote)
+
+                @pl.when(part == 0)
+                def _():
+                    pltpu.make_async_copy(rows, there, recv_sem.at[part]).start()
+            else:
+                remote()
+
+    def wait_sent(part):
+        @pl.when(part == 0)
+        def _():
+            rows = inbox.at[0, pl.ds(0, 7 * SLOTS)]
+            pltpu.make_async_copy(rows, rows, send_sem.at[0]).wait()
+
+        @pl.when(part != 0)
+        def _():
+            pltpu.make_async_copy(inbox.at[part], inbox.at[part], send_sem.at[part]).wait()
+
     pl.semaphore_wait(barrier, len(plane) + len(line))
     for device in line:
         pl.semaphore_signal(ready, inc=1, device_id=device, device_id_type=MESH)
-    rows_window(0)
+    feat_pad[W - 32 : W, :] = jnp.zeros((32, GRID), BF16)
+    copies[0].wait()
+    turn(sender, sender_turned)
+    copies[2].wait()
+    turn(length, length_turned)
+    copies[1].wait()
+    feat_pad[0:VARS, :] = feat[...]
+    gather_part(0)
     pl.semaphore_wait(ready, len(line))
-    send_window(0)
-
-    @pl.loop(1, 4)
-    def _(w):
-        pick_window(w)
-        rows_window(w)
-        send_window(w)
+    send_part(0)
+
+    @pl.loop(1, AHEAD)
+    def _(part):
+        gather_part(part)
+        send_part(part)
 
     for copy in copies[3:]:
         copy.wait()
@@ -161,56 +185,34 @@
         for k in range(M // TILE):
             hit = ids == lanes((TILE, TILE)) + k * TILE
             halo_pick[i * TILE : (i + 1) * TILE, k * TILE : (k + 1) * TILE] = hit.astype(F32).astype(BF16)
+    turn(target, target_turned)
     summed[...] = jnp.zeros((M, D), F32)
     ends = (M + 4 * HALO) * 4 + 8
     table[0:8, :] = jnp.zeros((8, TILE), F32)
     table[ends : ends + 8, :] = jnp.zeros((8, TILE), F32)
 
-    for q in range(4):
-        turned[q] = pltpu.roll(target[...], (4 - z + q) % 4 * SLOTS, 1)
-
-    def scatter_part(w, dz):
-        back = (4 - dz) % 4
-        block = lanes((1, TILE)) // SLOTS
-        for h in range(2):
-            ids = None
-            for p in range(4):
-                i, j = (h * 4 + p) // 2, p % 2
-                source = ((x + 4 - i) % 4 * 4 + (y + 8 - i - w) % 4) * 2 + (core + j) % 2
-                row = turned[(p - back) % 4, pl.ds(source, 1), :]
-                ids = row if ids is None else jnp.where(block == p, row, ids)
-            ids = jnp.broadcast_to(ids, (TILE, TILE))
-            at = dz * CHUNK + h * TILE
+    @pl.loop(0, 16)
+    def _(part):
+        wait_sent(part)
+
+        @pl.when(part + AHEAD < 16)
+        def _():
+            gather_part(part + AHEAD)
+            send_part(part + AHEAD)
+
+        for half in range(2):
+            ids = jnp.broadcast_to(pieces(target_turned, part, half, -1), (TILE, TILE))
             for k in range(M // TILE):
                 hit = ids == lax.broadcasted_iota(jnp.int32, (TILE, TILE), 0) + k * TILE
-                scatter[k * TILE : (k + 1) * TILE, at : at + TILE] = hit.astype(F32).astype(BF16)
-
-    def messages_part(w, dz):
-        part = inbox.at[w * 4 + dz]
-        pltpu.make_async_copy(part, part, recv_sem.at[w * 4 + dz]).wait()
-        first = dot(part[...].reshape(CHUNK, W), wcat[...])
+                scatter[k * TILE : (k + 1) * TILE, half * TILE : (half + 1) * TILE] = hit.astype(F32).astype(BF16)
+        pltpu.make_async_copy(inbox.at[part], inbox.at[part], recv_sem.at[part]).wait()
+        first = dot(inbox[part], wcat[...])
         latent = half_silu(first[:, :D]).astype(BF16)
         pre = dot(latent, wsend[...]) * 0.5 + first[:, D:]
-        msgs[dz * CHUNK : (dz + 1) * CHUNK, :] = half_silu(pre).astype(BF16)
-
-    def add_parts(lo, hi):
+        msgs[...] = half_silu(pre).astype(BF16)
         for k in range(M // CHUNK):
             rows = slice(k * CHUNK, (k + 1) * CHUNK)
-            summed[rows, :] += dot(scatter[rows, lo * CHUNK : hi * CHUNK], msgs[lo * CHUNK : hi * CHUNK, :])
-
-    @pl.loop(0, 3)
-    def _(w):
-        for dz in range(4):
-            scatter_part(w, dz)
-        for dz in range(4):
-            messages_part(w, dz)
-        add_parts(0, 4)
-
-    for dz in range(4):
-        scatter_part(3, dz)
-    for dz in range(4):
-        messages_part(3, dz)
-        add_parts(dz, dz + 1)
+            summed[rows, :] += dot(scatter[rows, :], msgs[...])
 
     for k in range(M // CHUNK):
         rows = slice(k * CHUNK, (k + 1) * CHUNK)
@@ -279,10 +281,6 @@
     result = pltpu.make_async_copy(ext, out_hbm, out_sem)
     result.start()
     result.wait()
-    for s in range(15):
-        pltpu.make_async_copy(inbox.at[s], inbox.at[s], send_sem.at[0]).wait()
-    sent = inbox.at[15, pl.ds(0, 7)]
-    pltpu.make_async_copy(sent, sent, send_sem.at[0]).wait()
 
 
 def on_device(
@@ -298,12 +296,14 @@
     scratch = [
         VM((W, GRID), BF16),
         VM((W, 2 * D), BF16),
-        VM((8 * TILE, GRID), BF16),
-        VM((32, TILE, W), BF16),
-        VM((16, 8, SLOTS, W), BF16),
+        VM((CHUNK, GRID), BF16),
+        VM((16, CHUNK, W), BF16),
+        VM((16, CHUNK, W), BF16),
         VM((4, 32, TILE), jnp.int32),
-        VM((M, 4 * CHUNK), BF16),
-        VM((4 * CHUNK, D), BF16),
+        VM((4, 32, TILE), F32),
+        VM((4, 32, TILE), jnp.int32),
+        VM((M, CHUNK), BF16),
+        VM((CHUNK, D), BF16),
         VM((M, D), F32),
         VM((M, D), BF16),
         VM((4 * HALO, M), BF16),
@@ -318,7 +318,7 @@
         pltpu.SMEM((DEG * M,), jnp.int32),
         pltpu.SemaphoreType.DMA((len(args),)),
         pltpu.SemaphoreType.DMA,
-        pltpu.SemaphoreType.DMA((1,)),
+        pltpu.SemaphoreType.DMA((16,)),
         pltpu.SemaphoreType.DMA((16,)),
         pltpu.SemaphoreType.DMA((LAYERS, 4)),
         pltpu.SemaphoreType.DMA((LAYERS, 4)),

time: 72.6 us -> 71.3 us (0.982); the launches traced: 71.4 us -> 71.2 us
  no operation moved by 1% of the time
where the time goes in v3:
time: 71.3 us; the launch traced here: 71.2 us
  Pallas kernels  68.9 us (97%)
  local copies, waits for them, and re-layouts  2.26 us (3%)
    pallas_call x1, Pallas kernels, on_device(): pl.pallas_call(kernel, out_shape=jax.ShapeDtypeStruct((M, D), BF16), in_s...  68.9 us
    unnamed x1, local copies, waits for them, and re-layouts  2.26 us

profile of v3, /device:TPU:2, one launch (start us, length us, event | category | flops | bytes accessed | tf_op | source)
XLA Modules:
  0.0 71.2 jit_solution(8740842015679001394)
XLA Ops:
  0.0 68.9 %shard_map.145 = bf16[1024,512]{1,0:T(8,128)(2,1)} custom-call(bf16[227,2048]{1,0:T(8,128)(2,1)} %bitcast.6, bf16[227,512]{1,0:T(8,128)(2,1)} %embed_hbm.1, bf16[512,512]{1,0:T(8,128)(2,1)} %send_hbm.1, bf16[512]{0:T(512)(128)(2,1)} %vec_hbm.1, s32[32,128]{1,0:T(8,128)} %bitcast.8, f32[32,128]{1,0:T(8,128)} %bitcast.9, s32[32,128]{1,0:T(8,128)} %bitcast.10, ...), custom_call_target="tpu_custom_call" | custom-call | tf_op jit(solution)/shard_map/pallas_call | solution.py:329
  68.9 2.3 %copy.17 = bf16[1024,512]{1,0:T(8,128)(2,1)} copy(bf16[1024,512]{1,0:T(8,128)(2,1)} %shard_map.145) | data formatting | bytes 2097152

commit v4 on v3

--- a/solution.py
+++ b/solution.py
@@ -15,6 +15,7 @@
 CHUNK = 256
 PAIRS = 16
 AHEAD = 6
+STEP = 2
 
 
 def dot(a, b):
@@ -45,7 +46,7 @@
     out_hbm,
     feat, embed, wsend, vec, sender, length, target, wagg, halo_ids, src, wsrc, wdst, wup, wdown, gain,
     feat_pad, wcat, pick, outbox, inbox, sender_turned, length_turned, target_turned, scatter, msgs, summed, ext, halo_pick, halo_out, halo_in,
-    table, recv, sums, esum, up, src_v, src_s,
+    halo_now, halo_up, table, recv, sums, esum, up, src_v, src_s,
     in_sem, idx_sem, send_sem, recv_sem, halo_send, halo_recv, out_sem, ready,
 ):
     band, z = lax.axis_index("band"), lax.axis_index("patch")
@@ -191,68 +192,73 @@
     table[0:8, :] = jnp.zeros((8, TILE), F32)
     table[ends : ends + 8, :] = jnp.zeros((8, TILE), F32)
 
-    @pl.loop(0, 16)
-    def _(part):
-        wait_sent(part)
-
-        @pl.when(part + AHEAD < 16)
+    @pl.loop(0, 16 // STEP)
+    def _(step):
+        for h in range(STEP):
+            wait_sent(step * STEP + h)
+
+        @pl.when(step * STEP + AHEAD < 16)
         def _():
-            gather_part(part + AHEAD)
-            send_part(part + AHEAD)
-
-        for half in range(2):
-            ids = jnp.broadcast_to(pieces(target_turned, part, half, -1), (TILE, TILE))
+            @pl.loop(0, STEP)
+            def _(h):
+                gather_part(step * STEP + AHEAD + h)
+                send_part(step * STEP + AHEAD + h)
+
+        for h in range(STEP * 2):
+            ids = jnp.broadcast_to(pieces(target_turned, step * STEP + h // 2, h % 2, -1), (TILE, TILE))
             for k in range(M // TILE):
                 hit = ids == lax.broadcasted_iota(jnp.int32, (TILE, TILE), 0) + k * TILE
-                scatter[k * TILE : (k + 1) * TILE, half * TILE : (half + 1) * TILE] = hit.astype(F32).astype(BF16)
-        pltpu.make_async_copy(inbox.at[part], inbox.at[part], recv_sem.at[part]).wait()
-        first = dot(inbox[part], wcat[...])
-        latent = half_silu(first[:, :D]).astype(BF16)
-        pre = dot(latent, wsend[...]) * 0.5 + first[:, D:]
+                scatter[k * TILE : (k + 1) * TILE, h * TILE : (h + 1) * TILE] = hit.astype(F32).astype(BF16)
+        for h in range(STEP):
+            part = step * STEP + h
+            pltpu.make_async_copy(inbox.at[part], inbox.at[part], recv_sem.at[part]).wait()
+        rows = inbox[pl.ds(step * STEP, STEP)].reshape(STEP * CHUNK, W)
+        latent = half_silu(dot(rows, wcat[:, :D])).astype(BF16)
+        pre = dot(latent, wsend[...]) * 0.5 + dot(rows[:, TILE:], wcat[TILE:, D:])
         msgs[...] = half_silu(pre).astype(BF16)
         for k in range(M // CHUNK):
             rows = slice(k * CHUNK, (k + 1) * CHUNK)
             summed[rows, :] += dot(scatter[rows, :], msgs[...])
 
-    for k in range(M // CHUNK):
-        rows = slice(k * CHUNK, (k + 1) * CHUNK)
-        ext[rows, :] = half_silu(dot(summed[rows, :].astype(BF16), wagg[...]) * 0.5).astype(BF16)
-    src_copy.wait()
-
     neighbours = ((band, (z + 1) % 4), (band, (z + 3) % 4), ((band + 1) % 32, z), ((band + 31) % 32, z))
     low = lax.broadcasted_iota(jnp.int32, (8, TILE), 0) < 4
 
-    @pl.loop(0, LAYERS)
-    def _(layer):
-        halos = []
+    def send_halos(layer, values):
+        copies = []
         for i in range(4):
             rows = slice(i * HALO, (i + 1) * HALO)
             if i % 2 == 0:
                 both = slice(i * HALO, (i + 2) * HALO)
-                halo_out[layer, both, :] = dot(halo_pick[both, :], ext[...]).astype(BF16)
+                halo_out[layer, both, :] = dot(halo_pick[both, :], values[...]).astype(BF16)
             copy = pltpu.make_async_remote_copy(
                 src_ref=halo_out.at[layer, rows], dst_ref=halo_in.at[layer, rows],
                 send_sem=halo_send.at[layer, i], recv_sem=halo_recv.at[layer, i],
                 device_id=neighbours[i], device_id_type=MESH,
             )
             copy.start()
-            halos.append(copy)
+            copies.append(copy)
+        return copies
+
+    def aggregated(sums_16):
+        return half_silu(dot(sums_16, wagg[...]) * 0.5).astype(BF16)
+
+    def updated(layer, own, first, sums_16):
+        hidden = half_silu((first + dot(sums_16, wup[layer, D : 2 * D, :])) * 0.5).astype(BF16)
+        mixed = dot(hidden, wdown[layer])
+        centre = mixed - jnp.mean(mixed, axis=1, keepdims=True)
+        spread = jnp.mean(centre * centre, axis=1, keepdims=True)
+        normed = centre * lax.rsqrt(spread + 1e-05) * gain[layer : layer + 1, :]
+        return (own.astype(F32) + normed).astype(BF16)
+
+    def project(layer):
         for k in range(M // CHUNK):
             rows = slice(k * CHUNK, (k + 1) * CHUNK)
             own = ext[rows, :]
             put_rows(table, 8 + k * CHUNK * 4, dot(own, wsrc[layer]) * 0.5)
             put_rows(recv, k * CHUNK * 4, dot(own, wdst[layer]) * 0.5)
             up[rows, :] = dot(own, wup[layer, 0:D, :])
-        for i in range(4):
-            halos[i].wait()
-            rows = slice(i * HALO, (i + 1) * HALO)
-            value = dot(halo_in[layer, rows, :], wsrc[layer]) * 0.5
-            if i == 2:
-                value = jnp.where(band == 0, 0.0, value)
-            if i == 3:
-                value = jnp.where(band == 31, 0.0, value)
-            put_rows(table, 8 + (M + i * HALO) * 4, value)
-
+
+    def edges():
         @pl.loop(0, M // 2 // PAIRS)
         def _(t):
             for u in range(PAIRS):
@@ -271,16 +277,47 @@
             rows = slice(k * CHUNK, (k + 1) * CHUNK)
             for j in range(D // TILE):
                 esum[rows, j * TILE : (j + 1) * TILE] = sums[pl.ds(k * CHUNK * 4 + j, CHUNK, stride=4), :].astype(BF16)
-            hidden = half_silu((up[rows, :] + dot(esum[rows, :], wup[layer, D : 2 * D, :])) * 0.5).astype(BF16)
-            mixed = dot(hidden, wdown[layer])
-            centre = mixed - jnp.mean(mixed, axis=1, keepdims=True)
-            spread = jnp.mean(centre * centre, axis=1, keepdims=True)
-            normed = centre * lax.rsqrt(spread + 1e-05) * gain[pl.ds(layer, 1), :]
-            ext[rows, :] = (ext[rows, :].astype(F32) + normed).astype(BF16)
-
-    result = pltpu.make_async_copy(ext, out_hbm, out_sem)
-    result.start()
-    result.wait()
+
+    def put_halo(layer, i, rows):
+        value = dot(rows, wsrc[layer]) * 0.5
+        if i == 2:
+            value = jnp.where(band == 0, 0.0, value)
+        if i == 3:
+            value = jnp.where(band == 31, 0.0, value)
+        put_rows(table, 8 + (M + i * HALO) * 4, value)
+
+    esum[...] = summed[...].astype(BF16)
+    halos = send_halos(0, esum)
+    for k in range(M // CHUNK):
+        rows = slice(k * CHUNK, (k + 1) * CHUNK)
+        ext[rows, :] = aggregated(esum[rows, :])
+    project(0)
+    src_copy.wait()
+    for i in (2, 3, 0, 1):
+        rows = slice(i * HALO, (i + 1) * HALO)
+        halos[i].wait()
+        halo_now[rows, :] = aggregated(halo_in[0, rows, :])
+        put_halo(0, i, halo_now[rows, :])
+    edges()
+
+    halos = send_halos(1, esum)
+    for k in range(M // CHUNK):
+        rows = slice(k * CHUNK, (k + 1) * CHUNK)
+        ext[rows, :] = updated(0, ext[rows, :], up[rows, :], esum[rows, :])
+    for k in range(2):
+        rows = slice(k * CHUNK, (k + 1) * CHUNK)
+        halo_up[rows, :] = dot(halo_now[rows, :], wup[0, 0:D, :])
+    project(1)
+    for i in (2, 3, 0, 1):
+        rows = slice(i * HALO, (i + 1) * HALO)
+        halos[i].wait()
+        put_halo(1, i, updated(0, halo_now[rows, :], halo_up[rows, :], halo_in[1, rows, :]))
+    edges()
+    for k in range(M // CHUNK):
+        rows = slice(k * CHUNK, (k + 1) * CHUNK)
+        ext[rows, :] = updated(1, ext[rows, :], up[rows, :], esum[rows, :])
+        pltpu.make_async_copy(ext.at[rows], out_hbm.at[rows], out_sem).start()
+    pltpu.make_async_copy(ext, out_hbm, out_sem).wait()
 
 
 def on_device(
@@ -302,13 +339,15 @@
         VM((4, 32, TILE), jnp.int32),
         VM((4, 32, TILE), F32),
         VM((4, 32, TILE), jnp.int32),
-        VM((M, CHUNK), BF16),
-        VM((CHUNK, D), BF16),
+        VM((M, STEP * CHUNK), BF16),
+        VM((STEP * CHUNK, D), BF16),
         VM((M, D), F32),
         VM((M, D), BF16),
         VM((4 * HALO, M), BF16),
         VM((LAYERS, 4 * HALO, D), BF16),
         VM((LAYERS, 4 * HALO, D), BF16),
+        VM((4 * HALO, D), BF16),
+        VM((4 * HALO, D), F32),
         VM(((M + 4 * HALO) * 4 + 16, TILE), F32),
         VM((M * 4, TILE), F32),
         VM((M * 4, TILE), F32),

time: 71.3 us -> 69.4 us (0.973)
  Pallas kernels: 68.9 us -> 66.3 us
    pallas_call x1, Pallas kernels: 68.9 us -> 66.3 us  [on_device(): pl.pallas_call(kernel, out_shape=jax.ShapeDtypeStruct((M, D), BF16), in_s...]
where the time goes in v4:
time: 69.4 us; the launch traced here: 68.6 us
  Pallas kernels  66.3 us (96%)
  local copies, waits for them, and re-layouts  2.26 us (3%)
    pallas_call x1, Pallas kernels, on_device(): pl.pallas_call(kernel, out_shape=jax.ShapeDtypeStruct((M, D), BF16), in_s...  66.3 us
    unnamed x1, local copies, waits for them, and re-layouts  2.26 us

profile of v4, /device:TPU:2, one launch (start us, length us, event | category | flops | bytes accessed | tf_op | source)
XLA Modules:
  0.0 68.6 jit_solution(6471550883720483815)
XLA Ops:
  0.0 66.3 %shard_map.145 = bf16[1024,512]{1,0:T(8,128)(2,1)} custom-call(bf16[227,2048]{1,0:T(8,128)(2,1)} %bitcast.6, bf16[227,512]{1,0:T(8,128)(2,1)} %embed_hbm.1, bf16[512,512]{1,0:T(8,128)(2,1)} %send_hbm.1, bf16[512]{0:T(512)(128)(2,1)} %vec_hbm.1, s32[32,128]{1,0:T(8,128)} %bitcast.8, f32[32,128]{1,0:T(8,128)} %bitcast.9, s32[32,128]{1,0:T(8,128)} %bitcast.10, ...), custom_call_target="tpu_custom_call" | custom-call | tf_op jit(solution)/shard_map/pallas_call | solution.py:368
  66.3 2.3 %copy.17 = bf16[1024,512]{1,0:T(8,128)(2,1)} copy(bf16[1024,512]{1,0:T(8,128)(2,1)} %shard_map.145) | data formatting | bytes 2097152

commit v5 on v4

--- a/solution.py
+++ b/solution.py
@@ -278,13 +278,14 @@
             for j in range(D // TILE):
                 esum[rows, j * TILE : (j + 1) * TILE] = sums[pl.ds(k * CHUNK * 4 + j, CHUNK, stride=4), :].astype(BF16)
 
-    def put_halo(layer, i, rows):
+    def put_halos(layer, i, rows):
         value = dot(rows, wsrc[layer]) * 0.5
+        below, above = value[:HALO], value[HALO:]
         if i == 2:
-            value = jnp.where(band == 0, 0.0, value)
-        if i == 3:
-            value = jnp.where(band == 31, 0.0, value)
-        put_rows(table, 8 + (M + i * HALO) * 4, value)
+            below = jnp.where(band == 0, 0.0, below)
+            above = jnp.where(band == 31, 0.0, above)
+        put_rows(table, 8 + (M + i * HALO) * 4, below)
+        put_rows(table, 8 + (M + (i + 1) * HALO) * 4, above)
 
     esum[...] = summed[...].astype(BF16)
     halos = send_halos(0, esum)
@@ -293,11 +294,12 @@
         ext[rows, :] = aggregated(esum[rows, :])
     project(0)
     src_copy.wait()
-    for i in (2, 3, 0, 1):
-        rows = slice(i * HALO, (i + 1) * HALO)
+    for i in (2, 0):
+        rows = slice(i * HALO, (i + 2) * HALO)
         halos[i].wait()
+        halos[i + 1].wait()
         halo_now[rows, :] = aggregated(halo_in[0, rows, :])
-        put_halo(0, i, halo_now[rows, :])
+        put_halos(0, i, halo_now[rows, :])
     edges()
 
     halos = send_halos(1, esum)
@@ -308,10 +310,11 @@
         rows = slice(k * CHUNK, (k + 1) * CHUNK)
         halo_up[rows, :] = dot(halo_now[rows, :], wup[0, 0:D, :])
     project(1)
-    for i in (2, 3, 0, 1):
-        rows = slice(i * HALO, (i + 1) * HALO)
+    for i in (2, 0):
+        rows = slice(i * HALO, (i + 2) * HALO)
         halos[i].wait()
-        put_halo(1, i, updated(0, halo_now[rows, :], halo_up[rows, :], halo_in[1, rows, :]))
+        halos[i + 1].wait()
+        put_halos(1, i, updated(0, halo_now[rows, :], halo_up[rows, :], halo_in[1, rows, :]))
     edges()
     for k in range(M // CHUNK):
         rows = slice(k * CHUNK, (k + 1) * CHUNK)

time: 69.4 us -> 68.1 us (0.981)
  Pallas kernels: 66.3 us -> 65 us
    pallas_call x1, Pallas kernels: 66.3 us -> 65 us  [on_device(): pl.pallas_call(kernel, out_shape=jax.ShapeDtypeStruct((M, D), BF16), in_s...]
where the time goes in v5:
time: 68.1 us; the launch traced here: 67.2 us
  Pallas kernels  65 us (95%)
  local copies, waits for them, and re-layouts  2.26 us (3%)
    pallas_call x1, Pallas kernels, on_device(): pl.pallas_call(kernel, out_shape=jax.ShapeDtypeStruct((M, D), BF16), in_s...  65 us
    unnamed x1, local copies, waits for them, and re-layouts  2.26 us

profile of v5, /device:TPU:2, one launch (start us, length us, event | category | flops | bytes accessed | tf_op | source)
XLA Modules:
  0.0 67.2 jit_solution(7275172308842435438)
XLA Ops:
  0.0 65.0 %shard_map.145 = bf16[1024,512]{1,0:T(8,128)(2,1)} custom-call(bf16[227,2048]{1,0:T(8,128)(2,1)} %bitcast.6, bf16[227,512]{1,0:T(8,128)(2,1)} %embed_hbm.1, bf16[512,512]{1,0:T(8,128)(2,1)} %send_hbm.1, bf16[512]{0:T(512)(128)(2,1)} %vec_hbm.1, s32[32,128]{1,0:T(8,128)} %bitcast.8, f32[32,128]{1,0:T(8,128)} %bitcast.9, s32[32,128]{1,0:T(8,128)} %bitcast.10, ...), custom_call_target="tpu_custom_call" | custom-call | tf_op jit(solution)/shard_map/pallas_call | solution.py:371
  65.0 2.3 %copy.17 = bf16[1024,512]{1,0:T(8,128)(2,1)} copy(bf16[1024,512]{1,0:T(8,128)(2,1)} %shard_map.145) | data formatting | bytes 2097152

commit v6 on v5

--- a/solution.py
+++ b/solution.py
@@ -13,6 +13,7 @@
 HALO, DEG, LAYERS = 128, 6, 2
 TILE = 128
 CHUNK = 256
+BIG = 512
 PAIRS = 16
 AHEAD = 6
 STEP = 2
@@ -216,8 +217,8 @@
         latent = half_silu(dot(rows, wcat[:, :D])).astype(BF16)
         pre = dot(latent, wsend[...]) * 0.5 + dot(rows[:, TILE:], wcat[TILE:, D:])
         msgs[...] = half_silu(pre).astype(BF16)
-        for k in range(M // CHUNK):
-            rows = slice(k * CHUNK, (k + 1) * CHUNK)
+        for k in range(M // BIG):
+            rows = slice(k * BIG, (k + 1) * BIG)
             summed[rows, :] += dot(scatter[rows, :], msgs[...])
 
     neighbours = ((band, (z + 1) % 4), (band, (z + 3) % 4), ((band + 1) % 32, z), ((band + 31) % 32, z))
@@ -251,11 +252,11 @@
         return (own.astype(F32) + normed).astype(BF16)
 
     def project(layer):
-        for k in range(M // CHUNK):
-            rows = slice(k * CHUNK, (k + 1) * CHUNK)
+        for k in range(M // BIG):
+            rows = slice(k * BIG, (k + 1) * BIG)
             own = ext[rows, :]
-            put_rows(table, 8 + k * CHUNK * 4, dot(own, wsrc[layer]) * 0.5)
-            put_rows(recv, k * CHUNK * 4, dot(own, wdst[layer]) * 0.5)
+            put_rows(table, 8 + k * BIG * 4, dot(own, wsrc[layer]) * 0.5)
+            put_rows(recv, k * BIG * 4, dot(own, wdst[layer]) * 0.5)
             up[rows, :] = dot(own, wup[layer, 0:D, :])
 
     def edges():

time: 68.1 us -> 68.1 us (level)
  no operation moved by 1% of the time
where the time goes in v6:
time: 68.1 us; the launch traced here: 67.2 us
  Pallas kernels  65 us (95%)
  local copies, waits for them, and re-layouts  2.26 us (3%)
    pallas_call x1, Pallas kernels, on_device(): pl.pallas_call(kernel, out_shape=jax.ShapeDtypeStruct((M, D), BF16), in_s...  65 us
    unnamed x1, local copies, waits for them, and re-layouts  2.26 us

profile of v6, /device:TPU:2, one launch (start us, length us, event | category | flops | bytes accessed | tf_op | source)
XLA Modules:
  0.0 67.2 jit_solution(13596444768671918603)
XLA Ops:
  0.0 65.0 %shard_map.145 = bf16[1024,512]{1,0:T(8,128)(2,1)} custom-call(bf16[227,2048]{1,0:T(8,128)(2,1)} %bitcast.6, bf16[227,512]{1,0:T(8,128)(2,1)} %embed_hbm.1, bf16[512,512]{1,0:T(8,128)(2,1)} %send_hbm.1, bf16[512]{0:T(512)(128)(2,1)} %vec_hbm.1, s32[32,128]{1,0:T(8,128)} %bitcast.8, f32[32,128]{1,0:T(8,128)} %bitcast.9, s32[32,128]{1,0:T(8,128)} %bitcast.10, ...), custom_call_target="tpu_custom_call" | custom-call | tf_op jit(solution)/shard_map/pallas_call | solution.py:372
  65.0 2.3 %copy.17 = bf16[1024,512]{1,0:T(8,128)(2,1)} copy(bf16[1024,512]{1,0:T(8,128)(2,1)} %shard_map.145) | data formatting | bytes 2097152
